TPU v7x, 256 devices: a whole 4x4x8 slice. The times are simulated.
256 devices in a mesh: row: 8 (over z), col: 16 (over y, x), layer: 2 (over core).
Axes of the slice: x: 4, y: 4, z: 8, core: 2. Of those that a mesh axis runs over, the one named last changes fastest.
Arguments:
- density: bfloat16 [8192, 8192], P('row', ('col', 'layer')), may hold values from -3 to 3
- block_mask: int32 [64, 64], P('row', ('col', 'layer')), may hold values from 0 to 1, as said below
- keep_mask: int32 [64, 64], P('row', ('col', 'layer')), may hold values 0 or 1
- branch_flag: int32 [64], P('row'), may hold values from 0 to 1
Outputs:
- updated: float32 [8192, 8192], P('row', ('col', 'layer'))
- trace_new: float32 [], replicated
Inputs may be any that keep to these rules, and one draw needn't show every extreme that they name: `block_mask`: symmetric, 1 on the diagonal; 1 where two blocks' centres in a periodic box lie within a cutoff distance of each other, else 0; block labels are in no spatial order. `keep_mask`: 0 or 1 for each block.
All inputs are finite; a program needn't handle non-finite values.
Results may differ from a plain program's by a relative error of at most 0.0004.
Values may be sent and summed in bfloat16 or wider, within the bound.
No kernel may reach another device: no remote copies, remote signals or barrier semaphores. Data moves between devices by JAX's collectives and lax.ppermute only.
A program may use at most 64 MiB of HBM per device.

v0:
```python
import functools

import jax
import jax.numpy as jnp
from jax import lax
from jax.sharding import Mesh
from jax.sharding import PartitionSpec as P

BLK = 128
COL = ("col_0", "col_1")
ROW_COL_LAYER = ("row", "col_0", "col_1", "layer")
COL_LAYER = ("col_0", "col_1", "layer")


def partner(value, axis, stride):
    mask = 2**stride
    pairs = [(source, source ^ mask) for source in range(lax.axis_size(axis))]
    return lax.ppermute(value, axis, pairs)


def split_up(value, dim, devices):
    shape = value.shape
    pieces = value.reshape(*shape[:dim], devices, shape[dim] // devices, *shape[dim + 1 :])
    return jnp.moveaxis(pieces, dim, 0)


def sum_at_owner(value, axis, dim):
    devices = lax.axis_size(axis)
    pieces = lax.all_to_all(split_up(value, dim, devices), axis, 0, 0, tiled=True)
    return jnp.sum(pieces, axis=0)


def over_axes(value, axes):
    return functools.reduce(lax.psum, axes, value)


def expand_mask(block_mask):
    return jnp.repeat(jnp.repeat(block_mask, BLK, axis=0), BLK, axis=1)


def on_device(density, block_mask, keep_mask, branch_flag):
    row_count = density.shape[0]
    col_width = density.shape[1]
    masked = density * expand_mask(block_mask).astype(jnp.bfloat16)
    col_panel = lax.all_gather(masked, "row", axis=0, tiled=True)
    layer_index = lax.axis_index("layer")
    col_groups = lax.axis_size(COL)
    grouped = col_panel.reshape(col_groups, 2, col_width, col_width)
    own_rows = lax.dynamic_index_in_dim(grouped, layer_index, 1, keepdims=False)
    outgoing = lax.dynamic_index_in_dim(grouped, 1 - layer_index, 1, keepdims=False)
    peer_rows = partner(outgoing, "layer", 0)
    own_rows = own_rows.reshape(col_groups * col_width, col_width)
    peer_rows = peer_rows.reshape(col_groups * col_width, col_width)
    lead_part = jnp.where(layer_index == 0, own_rows, peer_rows)
    tail_part = jnp.where(layer_index == 0, peer_rows, own_rows)
    inner_panel = jnp.concatenate([lead_part, tail_part], axis=1)
    partial_value = jnp.dot(
        lax.all_gather(masked, COL, axis=1, tiled=True),
        inner_panel,
        preferred_element_type=jnp.float32,
    )
    product = sum_at_owner(partial_value, "layer", 1)
    doubled = 2.0 * masked.astype(jnp.float32) - product
    flag_rows = jnp.repeat(branch_flag, BLK)[:, None]
    chosen = jnp.where(flag_rows == 1, product, doubled)
    updated = chosen * expand_mask(keep_mask).astype(jnp.float32)
    row_anchor = lax.axis_index("row") * row_count
    col_anchor = (
        lax.axis_index(COL) * lax.axis_size("layer") + lax.axis_index("layer")
    ) * col_width
    row_ids = row_anchor + jnp.arange(row_count, dtype=jnp.int32)[:, None]
    col_ids = col_anchor + jnp.arange(col_width, dtype=jnp.int32)[None, :]
    local_trace = jnp.sum(jnp.where(row_ids == col_ids, updated, 0.0))
    trace_new = over_axes(local_trace, ROW_COL_LAYER)
    return (updated, trace_new)


def solution(mesh):
    split = Mesh(
        mesh.devices.reshape(mesh.shape["row"], 4, 4, mesh.shape["layer"]),
        ("row", "col_0", "col_1", "layer"),
    )
    in_specs = (P("row", COL_LAYER), P("row", COL_LAYER), P("row", COL_LAYER), P("row"))
    out_specs = (P("row", COL_LAYER), P())
    return jax.shard_map(
        on_device, mesh=split, in_specs=in_specs, out_specs=out_specs, check_vma=False
    )
```

profile of v0, /device:TPU:1, one launch (start us, length us, event | category | flops | bytes accessed | tf_op | source)
XLA Modules:
  0.0 212.9 jit_solution(15898853218652076611)
XLA Ops:
  7.2 0.0 all-gather.5.cloned.1.call-start
  7.2 1.2 copy.10
  8.5 0.7 convert_element_type.25
  9.1 0.1 broadcast_bitcast_fusion.1
  9.2 0.8 bitcast_multiply_fusion
  10.1 0.0 all-gather.5.cloned.1.call-update
  10.1 0.0 all-gather.3.cloned.1.call-start
  10.1 0.7 all-gather.3.cloned.1.call-update
  10.9 58.0 %all-gather.5.cloned.1.call-done = bf16[8192,256]{0,1:T(8,128)(2,1)} async-done(((bf16[1024,256]{0,1:T(8,128)(2,1)}), bf16[8192,256]{0,1:T(8,128)(2,1)}) %all-gather.5.cloned.1.call-update) | async-done | bytes 4194320 | tf_op jit(solution)/shard_map/all_gather | solution.py:45
  68.9 7.8 %reshape.44 = bf16[16,2,256,256]{2,1,0,3:T(2,128)(2,1)} reshape(bf16[8192,256]{0,1:T(8,128)(2,1)} %all-gather.5.cloned.1.call-done) | data formatting | bytes 8388608 | tf_op jit(solution)/shard_map/reshape | solution.py:48
  76.7 13.4 %constant_dynamic-slice_fusion.1 = (bf16[16,1,256,256]{2,1,0,3:T(2,128)(2,1)}, bf16[16,1,256,256]{2,1,0,3:T(2,128)(2,1)}) fusion(bf16[16,2,256,256]{2,1,0,3:T(2,128)(2,1)} %reshape.44, s32[]{:T(128)S(6)} %select_n.28, s32[]{:T(128)S(6)} %select_n.29), kind=kLoop, calls=%fused_computation.18 | loop fusion | bytes 8388616 | tf_op jit(solution)/shard_map/jit(dynamic_index_in_dim)/dynamic_slice | solution.py:49
  90.1 0.0 copy-start.1
  90.1 0.0 copy-start.2
  90.1 10.5 %copy.15 = bf16[16,1,256,256]{3,2,0,1:T(8,128)(2,1)} copy(bf16[16,1,256,256]{2,1,0,3:T(2,128)(2,1)} %get-tuple-element.11) | data formatting | bytes 4194304
  100.6 0.7 collective-permute-start
  101.3 0.0 copy-done.1
  101.3 0.1 broadcast_bitcast_fusion
  101.4 0.0 copy-done.2
  101.4 0.1 broadcast_bitcast_fusion.2
  101.5 9.0 %copy.14 = bf16[16,1,256,256]{3,2,0,1:T(8,128)(2,1)S(1)} copy(bf16[16,1,256,256]{2,1,0,3:T(2,128)(2,1)} %get-tuple-element.10) | data formatting | bytes 4194304
  110.5 0.0 collective-permute-done
  110.5 3.8 %bitcast_select_fusion.1 = (bf16[4096,256]{1,0:T(8,128)(2,1)}, bf16[4096,256]{1,0:T(8,128)(2,1)}) fusion(bf16[16,256,256]{2,1,0:T(8,128)(2,1)} %collective-permute-done, bf16[16,1,256,256]{3,2,0,1:T(8,128)(2,1)S(1)} %copy.14, pred[]{:T(512)S(6)} %eq.35), kind=kLoop, calls=%fused_computation.5 | loop fusion | flops 2097152 | bytes 8388609 | tf_op jit(solution)/shard_map/jit(_where)/select_n | solution.py:54
  114.3 31.4 %all-gather.3.cloned.1.call-done = bf16[1024,4096]{0,1:T(8,128)(2,1)} async-done(((bf16[1024,256]{0,1:T(8,128)(2,1)}), bf16[1024,4096]{0,1:T(8,128)(2,1)}) %all-gather.3.cloned.1.call-update) | async-done | bytes 8388624 | tf_op jit(solution)/shard_map/all_gather | solution.py:58
  145.7 8.3 %fusion = f32[1024,512]{0,1:T(8,128)S(1)} fusion(bf16[1024,4096]{0,1:T(8,128)(2,1)} %all-gather.3.cloned.1.call-done, bf16[4096,256]{1,0:T(8,128)(2,1)} %get-tuple-element.9, bf16[4096,256]{1,0:T(8,128)(2,1)} %get-tuple-element.8), kind=kOutput, calls=%fused_computation | convolution fusion | flops 4303355904 | bytes 14680064 | tf_op jit(solution)/shard_map/dot_general | solution.py:57
  154.0 0.0 copy-start
  154.0 5.8 %all_to_all.5 = f32[2,1024,256]{1,2,0:T(8,128)S(1)} all-to-all(f32[2,1024,256]{1,2,0:T(8,128)S(1)} %bitcast.34), channel_id=1, replica_groups=mesh['row'=8,'col_0'=4,'col_1'=4,'layer'=2] {'layer'}, dimensions={0} | all-to-all | bytes 4194304 | tf_op jit(solution)/shard_map/all_to_all | solution.py:29
  159.8 1.2 reduce_sum.18
  161.0 0.0 copy-done
  161.0 2.3 %select_reduce_fusion = (f32[]{:T(128)}, f32[1024,256]{0,1:T(8,128)S(1)}) fusion(s32[1024]{0:T(1024)S(1)} %iota_add_fusion, s32[256]{0:T(256)S(1)} %iota_add_fusion.1, f32[1024,2]{0,1:T(2,128)S(1)} %bitcast.35, f32[1024,256]{0,1:T(8,128)} %reduce_sum.18, bf16[1024,256]{0,1:T(8,128)(2,1)S(1)} %copy-done, pred[1024]{0:T(1024)(128)(4,1)S(1)} %broadcast_bitcast_fusion.2), kind=kLoop, calls=%fused_computation.8 | loop fusion | flops 2097151 | bytes 2635780 | tf_op jit(solution)/shard_map/reduce_sum | solution.py:73
  163.3 14.6 %psum.28 = f32[]{:T(128)} all-reduce(f32[]{:T(128)} %get-tuple-element.6), channel_id=1, replica_groups=mesh['row'=8,'col_0'=4,'col_1'=4,'layer'=2] {'row'}, use_global_device_ids=true, to_apply=%region_2.3 | all-reduce | flops 1 | bytes 8 | tf_op jit(solution)/shard_map/psum | solution.py:34
  178.0 9.0 %psum.29 = f32[]{:T(128)} all-reduce(f32[]{:T(128)} %psum.28), channel_id=1, replica_groups=mesh['row'=8,'col_0'=4,'col_1'=4,'layer'=2] {'col_0'}, use_global_device_ids=true, to_apply=%region_3.4 | all-reduce | flops 1 | bytes 8 | tf_op jit(solution)/shard_map/psum | solution.py:34
  187.0 7.2 %psum.30 = f32[]{:T(128)} all-reduce(f32[]{:T(128)} %psum.29), channel_id=1, replica_groups=mesh['row'=8,'col_0'=4,'col_1'=4,'layer'=2] {'col_1'}, use_global_device_ids=true, to_apply=%region_4.5 | all-reduce | flops 1 | bytes 8 | tf_op jit(solution)/shard_map/psum | solution.py:34
  194.2 1.3 copy.13
  195.5 10.6 %psum.31 = f32[]{:T(128)} all-reduce(f32[]{:T(128)} %psum.30), channel_id=1, replica_groups=mesh['row'=8,'col_0'=4,'col_1'=4,'layer'=2] {'layer'}, use_global_device_ids=true, to_apply=%region_5.6 | all-reduce | flops 1 | bytes 8 | tf_op jit(solution)/shard_map/psum | solution.py:34
  (6 shorter events, 0.0 us)
Async XLA Ops:
  7.2 61.7 %all-gather.5.cloned.1.call-start = ((), (), s32[]{:S(2)}) async-start(), calls=%async_computation.2 | async-start | bytes 4718592 | tf_op jit(solution)/shard_map/all_gather | solution.py:45
  10.1 135.6 %all-gather.3.cloned.1.call-start = ((), (), s32[]{:S(2)}) async-start(), calls=%async_computation.1 | async-start | bytes 8912896 | tf_op jit(solution)/shard_map/all_gather | solution.py:58
  90.1 11.2 %copy-start.1 = (s32[8,2]{0,1:T(2,128)S(1)}, s32[8,2]{0,1:T(2,128)}, u32[]{:S(2)}) copy-start(s32[8,2]{0,1:T(2,128)} %param.6) | copy-start | bytes 196
  90.1 11.3 %copy-start.2 = (s32[8]{0:T(128)S(1)}, s32[8]{0:T(128)}, u32[]{:S(2)}) copy-start(s32[8]{0:T(128)} %param.7) | copy-start | bytes 100
  100.6 9.8 %collective-permute-start = (bf16[16,256,256]{2,1,0:T(8,128)(2,1)}, bf16[16,256,256]{2,1,0:T(8,128)(2,1)}, u32[]{:S(2)}, u32[]{:S(2)}) collective-permute-start(bf16[16,256,256]{2,1,0:T(8,128)(2,1)} %bitcast.3), channel_id=1, source_target_pairs={{0,1},{1,0},{2,3},{3,2},{4,5},{5,4},{6,7},{7,6},{8,9},{9,8},{10,11... | collective-permute-start | bytes 6291464 | tf_op jit(solution)/shard_map/ppermute | solution.py:18
  154.0 7.1 %copy-start = (bf16[1024,256]{0,1:T(8,128)(2,1)S(1)}, bf16[1024,256]{0,1:T(8,128)(2,1)}, u32[]{:S(2)}) copy-start(bf16[1024,256]{0,1:T(8,128)(2,1)} %bitcast_multiply_fusion) | copy-start | bytes 1572868
Sparse Core Ops, SparseCore 0:
  10.2 58.6 all-gather.4
  71.3 74.3 all-gather.2
where the time goes:
time: 214 us; the launch traced here: 213 us
  waiting for transfers between devices  90.1 us (42%)
  blocking collectives  47.2 us (22%)
  local copies, waits for them, and re-layouts  43.5 us (20%)
  between operations  14.1 us (7%)
  other arithmetic  8.9 us (4%)
  matrix products  8.26 us (4%)
    all_gather x1, waiting for transfers between devices, on_device(): col_panel = lax.all_gather(masked, 'row', axis=0, tiled=True)  58 us
    psum x4, blocking collectives, over_axes(): return functools.reduce(lax.psum, axes, value)  41.4 us
    all_gather x1, waiting for transfers between devices, on_device(): lax.all_gather(masked, COL, axis=1, tiled=True)  31.4 us
    unnamed x14, local copies, waits for them, and re-layouts  22.2 us
    dynamic_slice x1, local copies, waits for them, and re-layouts, on_device(): own_rows = lax.dynamic_index_in_dim(grouped, layer_index, 1, keepdims=False)  13.4 us
    dot_general x1, matrix products, on_device(): jnp.dot(lax.all_gather(masked, COL, axis=1, tiled=True), inner_panel, pre...  8.26 us
    reshape x1, local copies, waits for them, and re-layouts, on_device(): grouped = col_panel.reshape(col_groups, 2, col_width, col_width)  7.82 us
    all_to_all x1, blocking collectives, sum_at_owner(): lax.all_to_all(split_up(value, dim, devices), axis, 0, 0, tiled=True)  5.85 us
  transfers between devices with their start and end apart: 3, of which 2 were waited for; matrix products, arithmetic and copies ran while one was open for 21% of the time, Pallas kernels for 0%

commit v1 on v0

v1 whole, which is shorter than its diff:
```python
import functools

import jax
import jax.numpy as jnp
from jax import lax
from jax.experimental import pallas as pl
from jax.experimental.pallas import tpu as pltpu
from jax.sharding import Mesh
from jax.sharding import PartitionSpec as P

BLK = 128
Y, X = "col_0", "col_1"
COL_LAYER = (Y, X, "layer")
SMEM = pl.BlockSpec(memory_space=pltpu.SMEM)
VMEM = pl.BlockSpec(memory_space=pltpu.VMEM)
HBM = pl.BlockSpec(memory_space=pl.ANY)
PARAMS = pltpu.CompilerParams(vmem_limit_bytes=48 * 1024 * 1024)
ORDER4 = (0, -1, 1, 2)


def shift(value, axis, off):
    n = lax.axis_size(axis)
    return lax.ppermute(value, axis, [(i, (i + off) % n) for i in range(n)])


def ring4(own, axis):
    half = own.shape[0] // 2
    plus, minus = shift(own, axis, 1), shift(own, axis, -1)
    return plus, minus, shift(plus[:half], axis, 1), shift(minus[half:], axis, -1)


def ring8(own, axis):
    half = own.shape[0] // 2
    plus, minus = [own], [own]
    for _ in range(3):
        plus.append(shift(plus[-1], axis, 1))
        minus.append(shift(minus[-1], axis, -1))
    far = (shift(plus[-1][:half], axis, 1), shift(minus[-1][half:], axis, -1))
    return plus[1:], minus[1:], far


def mask_kernel(pos, bm, x, m, top, low, own, peer):
    layer = pos[3]
    rows = []
    for i in range(8):
        parts = [
            x[pl.ds(i * BLK, BLK), pl.ds(j * BLK, BLK)] * bm[i, j].astype(jnp.float32).astype(jnp.bfloat16)
            for j in range(2)
        ]
        rows.append(jnp.concatenate(parts, axis=1))
    for i in range(8):
        m[pl.ds(i * BLK, BLK), :] = rows[i]
        half = top if i < 4 else low
        half[pl.ds((i % 4) * BLK, BLK), :] = rows[i]
        at, cls, inner = i // 4, (i // 2) % 2, i % 2

        @pl.when(layer == cls)
        def _():
            own[at, pl.ds(inner * BLK, BLK), :] = rows[i]

        @pl.when(layer != cls)
        def _():
            peer[at, pl.ds(inner * BLK, BLK), :] = rows[i]


def place(pos, d, half):
    r, y, x = pos[0], pos[1], pos[2]
    src = lax.rem(r - d + 8, 8)
    col = src * 2 + half
    dy, dx = lax.rem(col // 4 - y + 4, 4), lax.rem(lax.rem(col, 4) - x + 4, 4)
    rank = lambda o: jnp.where(o == 0, 0, jnp.where(o == 3, 1, jnp.where(o == 1, 2, 3)))
    return rank(dy), rank(dx)


def load_b(pos, z_refs, by, bx, sems):
    copies = []
    pieces = [(d, ch, rh, z_refs[d].at[2 * ch + rh]) for d in range(4) for ch in range(2) for rh in range(2)]
    pieces += [(-d, ch, rh, z_refs[3 + d].at[2 * ch + rh]) for d in range(1, 4) for ch in range(2) for rh in range(2)]
    pieces += [(4, ch, rh, z_refs[7 + ch].at[rh]) for ch in range(2) for rh in range(2)]
    for d, ch, rh, src in pieces:
        ry, rx = place(pos, d, rh)
        cols = pl.ds(ch * 256, 256)
        for dst, at in ((by, ry * 4 + rx), (bx, rx * 4 + ry)):
            copies.append(pltpu.make_async_copy(src, dst.at[pl.ds(pl.multiple_of(at * 256, 256), 256), cols], sems.at[len(copies)]))
    return copies


def near_kernel(pos, *refs):
    z_refs, (t0, t1, t2, l0, l1, l2) = refs[:9], refs[9:15]
    p_own, p_peer, by_out, bx_out = refs[15:19]
    by, bx, a_top, a_low, sem_b, sem_a, sem_o = refs[19:]
    copies = load_b(pos, z_refs, by, bx, sem_b)
    n = 0
    for dst, srcs in ((a_top, (t0, t1, t2)), (a_low, (l0, l1, l2))):
        for g, src in enumerate(srcs):
            for k in range(4):
                copies.append(
                    pltpu.make_async_copy(src.at[pl.ds(k * 512, 512), :], dst.at[:, pl.ds((4 * g + k) * 256, 256)], sem_a.at[n])
                )
                n += 1
    for c in copies:
        c.start()
    for c in copies:
        c.wait()
    outs = [
        pltpu.make_async_copy(by.at[pl.ds(3072, 1024), :], by_out, sem_o.at[0]),
        pltpu.make_async_copy(bx.at[pl.ds(3072, 1024), :], bx_out, sem_o.at[1]),
    ]
    for c in outs:
        c.start()
    for base, a, b in ((0, a_top, by), (512, a_low, bx)):

        @pl.loop(0, 2)
        def _(i):
            rows = pl.ds(pl.multiple_of(i * 256, 256), 256)
            to = pl.ds(pl.multiple_of(base + i * 256, 256), 256)
            out = jnp.dot(a[rows, :], b[pl.ds(0, 3072), :], preferred_element_type=jnp.float32)
            p_own[to, :] = out[:, :256]
            p_peer[to, :] = out[:, 256:]

    for c in outs:
        c.wait()


def far_kernel(by, bx, q_top0, q_top1, q_low0, q_low1, p_own, p_peer, o_own, o_peer):
    for base, qs, b in ((0, (q_top0, q_top1), by), (512, (q_low0, q_low1), bx)):
        for i in range(2):
            to = pl.ds(base + i * 256, 256)
            a = jnp.concatenate(
                [qs[k // 2][pl.ds((k % 2) * 512 + i * 256, 256), :] for k in range(4)], axis=1
            )
            out = jnp.dot(a, b[...], preferred_element_type=jnp.float32)
            o_peer[to, :] = p_peer[to, :] + out[:, 256:]
            o_own[to, :] = p_own[to, :] + out[:, :256]


def final_kernel(pos, keep, flag, own, recv, m, out, trace):
    first = (pos[1] * 8 + pos[2] * 2 + pos[3]) * 2 - pos[0] * 8
    total = jnp.zeros((BLK, BLK), jnp.float32)
    eye = lax.broadcasted_iota(jnp.int32, (BLK, BLK), 0) == lax.broadcasted_iota(jnp.int32, (BLK, BLK), 1)
    for i in range(8):
        take = flag[i] == 1
        sign, twice = jnp.where(take, 1.0, -1.0), jnp.where(take, 0.0, 2.0)
        for j in range(2):
            at = (pl.ds(i * BLK, BLK), pl.ds(j * BLK, BLK))
            square = own[at] + recv[at]
            value = (twice * m[at].astype(jnp.float32) + sign * square) * keep[i, j].astype(jnp.float32)
            out[at] = value
            here = (first + j == i).astype(jnp.float32)
            total = total + jnp.where(eye, value, 0.0) * here
    trace[...] = jnp.sum(total.reshape(16, 8, BLK), axis=0)


def bf16(*shape):
    return jax.ShapeDtypeStruct(shape, jnp.bfloat16)


def f32(*shape):
    return jax.ShapeDtypeStruct(shape, jnp.float32)


def sum_all(value):
    for axes, n in (((Y, X), 16), ("row", 8)):
        spread = jnp.broadcast_to(value[None], (n, 8, BLK))
        value = jnp.sum(lax.all_to_all(spread, axes, 0, 0), axis=0)
    return jnp.sum(value + lax.ppermute(value, "layer", [(0, 1), (1, 0)]))


def on_device(density, block_mask, keep_mask, branch_flag):
    pos = jnp.stack([lax.axis_index(a) for a in ("row", Y, X, "layer")]).astype(jnp.int32)
    swap = [(0, 1), (1, 0)]
    m, top, low, own_rows, peer_rows = pl.pallas_call(
        mask_kernel,
        out_shape=[bf16(1024, 256), bf16(512, 256), bf16(512, 256), bf16(2, 256, 256), bf16(2, 256, 256)],
        in_specs=[SMEM, SMEM, VMEM],
        out_specs=[VMEM] * 5,
        compiler_params=PARAMS,
        name="mask",
    )(pos, block_mask, density)
    other = lax.ppermute(peer_rows, "layer", swap)
    z_tile = jnp.concatenate([own_rows, other], axis=0)
    z_plus, z_minus, z_far = ring8(z_tile, "row")
    row_top = jnp.concatenate([top, *ring4(top, X)], axis=0)
    row_low = jnp.concatenate([low, *ring4(low, Y)], axis=0)
    top_p, top_m, top_q0, top_q1 = ring4(row_top, Y)
    low_p, low_m, low_q0, low_q1 = ring4(row_low, X)
    p_own, p_peer, by, bx = pl.pallas_call(
        near_kernel,
        out_shape=[f32(1024, 256), f32(1024, 256), bf16(1024, 512), bf16(1024, 512)],
        in_specs=[SMEM] + [HBM] * 15,
        out_specs=[VMEM, VMEM, HBM, HBM],
        scratch_shapes=[
            pltpu.VMEM((4096, 512), jnp.bfloat16),
            pltpu.VMEM((4096, 512), jnp.bfloat16),
            pltpu.VMEM((512, 3072), jnp.bfloat16),
            pltpu.VMEM((512, 3072), jnp.bfloat16),
            pltpu.SemaphoreType.DMA((64,)),
            pltpu.SemaphoreType.DMA((24,)),
            pltpu.SemaphoreType.DMA((2,)),
        ],
        compiler_params=PARAMS,
        name="near",
        cost_estimate=pl.CostEstimate(flops=3_200_000_000, bytes_accessed=12_000_000, transcendentals=0),
    )(pos, z_tile, *z_plus, *z_minus, *z_far, row_top, top_p, top_m, row_low, low_p, low_m)
    p_own, p_peer = pl.pallas_call(
        far_kernel,
        out_shape=[f32(1024, 256), f32(1024, 256)],
        in_specs=[VMEM] * 8,
        out_specs=[VMEM, VMEM],
        input_output_aliases={6: 0, 7: 1},
        compiler_params=PARAMS,
        name="far",
        cost_estimate=pl.CostEstimate(flops=1_100_000_000, bytes_accessed=4_000_000, transcendentals=0),
    )(by, bx, top_q0, top_q1, low_q0, low_q1, p_own, p_peer)
    recv = lax.ppermute(p_peer, "layer", swap)
    updated, local_trace = pl.pallas_call(
        final_kernel,
        out_shape=[f32(1024, 256), f32(8, BLK)],
        in_specs=[SMEM, SMEM, SMEM, VMEM, VMEM, VMEM],
        out_specs=[VMEM, VMEM],
        compiler_params=PARAMS,
        name="final",
    )(pos, keep_mask, branch_flag, p_own, recv, m)
    return (updated, sum_all(local_trace))


def solution(mesh):
    split = Mesh(
        mesh.devices.reshape(mesh.shape["row"], 4, 4, mesh.shape["layer"]),
        ("row", Y, X, "layer"),
    )
    in_specs = (P("row", COL_LAYER), P("row", COL_LAYER), P("row", COL_LAYER), P("row"))
    out_specs = (P("row", COL_LAYER), P())
    return jax.shard_map(
        on_device, mesh=split, in_specs=in_specs, out_specs=out_specs, check_vma=False
    )
```

time: 214 us -> 123 us (0.57)
  waiting for transfers between devices: 90.1 us -> 33.5 us
  starting transfers between devices: 0.75 us -> 44.3 us
  local copies, waits for them, and re-layouts: 43.5 us -> 4.19 us
  blocking collectives: 47.2 us -> 22.3 us
  Pallas kernels: 0 us -> 16.7 us
  between operations: 14.1 us -> 0.98 us
  matrix products: 8.26 us -> 0 us
  other arithmetic: 8.9 us -> 0.7 us
    all_gather x2 -> x0, waiting for transfers between devices: 89.4 us -> none  [the longest x1 58 us: on_device(): col_panel = lax.all_gather(masked, 'row', axis=0, tiled=True)]
    ppermute x1 -> x27, starting transfers between devices: 0.67 us -> 44.3 us  [the longest x24 32.7 us: shift(): return lax.ppermute(value, axis, [(i, (i + off) % n) for i in range(n)])]
    psum x4 -> x0, blocking collectives: 41.4 us -> none  [over_axes(): return functools.reduce(lax.psum, axes, value)]
    ppermute x1 -> x27, waiting for transfers between devices: 0.01 us -> 33.5 us  [the longest x24 29.1 us: shift(): return lax.ppermute(value, axis, [(i, (i + off) % n) for i in range(n)])]
    unnamed x14 -> x32, local copies, waits for them, and re-layouts: 22.2 us -> 3.92 us
    pallas_call x0 -> x4, Pallas kernels: none -> 16.7 us  [the longest x1 10.1 us: on_device(): pl.pallas_call(near_kernel, out_shape=[f32(1024, 256), f32(1024, 256), bf...]
    all_to_all x1 -> x2, blocking collectives: 5.85 us -> 22.3 us  [sum_all(): value = jnp.sum(lax.all_to_all(spread, axes, 0, 0), axis=0)]
    dynamic_slice x1 -> x0, local copies, waits for them, and re-layouts: 13.4 us -> none  [on_device(): own_rows = lax.dynamic_index_in_dim(grouped, layer_index, 1, keepdims=False)]
  transfers between devices with their start and end apart: 3 -> 27, of which waited for: 2 -> 9; matrix products, arithmetic and copies ran while one was open for 21% -> 0% of each run, Pallas kernels for 0% -> 8%
where the time goes in v1:
time: 123 us
  starting transfers between devices  44.3 us (36%)
  waiting for transfers between devices  33.5 us (27%)
  blocking collectives  22.3 us (18%)
  Pallas kernels  16.7 us (14%)
  local copies, waits for them, and re-layouts  4.19 us (3%)
    ppermute x24, starting transfers between devices, shift(): return lax.ppermute(value, axis, [(i, (i + off) % n) for i in range(n)])  32.7 us
    ppermute x24, waiting for transfers between devices, shift(): return lax.ppermute(value, axis, [(i, (i + off) % n) for i in range(n)])  29.1 us
    all_to_all x2, blocking collectives, sum_all(): value = jnp.sum(lax.all_to_all(spread, axes, 0, 0), axis=0)  22.3 us
    pallas_call x1, Pallas kernels, on_device(): pl.pallas_call(near_kernel, out_shape=[f32(1024, 256), f32(1024, 256), bf...  10.1 us
    ppermute x1, starting transfers between devices, on_device(): recv = lax.ppermute(p_peer, 'layer', swap)  5.05 us
    unnamed x32, local copies, waits for them, and re-layouts  3.92 us
    pallas_call x1, Pallas kernels, on_device(): pl.pallas_call(far_kernel, out_shape=[f32(1024, 256), f32(1024, 256)], in...  3.89 us
    ppermute x1, starting transfers between devices, on_device(): other = lax.ppermute(peer_rows, 'layer', swap)  3.33 us
  transfers between devices with their start and end apart: 27, of which 9 were waited for; matrix products, arithmetic and copies ran while one was open for 0% of the time, Pallas kernels for 8%

profile of v1, /device:TPU:1, one launch (start us, length us, event | category | flops | bytes accessed | tf_op | source)
XLA Modules:
  0.0 122.6 jit_solution(7293661853739941589)
XLA Ops:
  0.6 0.7 copy-done.9
  1.3 0.1 copy.10.bm
  1.4 0.1 pad_add_fusion.pos
  1.5 1.0 copy-done.1
  2.5 0.8 mask.1
  3.3 3.3 %collective-permute-start = (bf16[2,256,256]{2,1,0:T(8,128)(2,1)S(1)}, bf16[2,256,256]{2,1,0:T(8,128)(2,1)S(1)}, u32[]{:S(2)}, u32[]{:S(2)}) collective-permute-start(bf16[2,256,256]{2,1,0:T(8,128)(2,1)S(1)} %get-tuple-element.16), channel_id=1, source_target_pairs={{0,1},{1,0},{2,3},{3,2},{4,5},{5,4},{6,7},{7,6},{8,9},{9,8},{10,11... | collective-permute-start | bytes 786440 | tf_op jit(solution)/shard_map/ppermute | solution.py:180
  6.7 1.1 collective-permute-done
  7.9 0.1 collective-permute-start.1
  7.9 1.2 collective-permute-start.15
  9.1 4.0 %collective-permute-start.4 = (bf16[4,256,256]{2,1,0:T(8,128)(2,1)S(1)}, bf16[4,256,256]{2,1,0:T(8,128)(2,1)S(1)}, u32[]{:S(2)}, u32[]{:S(2)}) collective-permute-start(bf16[4,256,256]{2,1,0:T(8,128)(2,1)S(1)} %constant_dynamic-update-slice_fusion.refs_0_), channel_id=1, source_target_pairs={{0,224},{32,0},{64,32},{96,64},{128,96},{160,128},{192,160},{224,1... | collective-permute-start | bytes 1572872 | tf_op jit(solution)/shard_map/ppermute | solution.py:23
  13.2 1.5 %collective-permute-start.16 = (bf16[512,256]{1,0:T(8,128)(2,1)S(1)}, bf16[512,256]{1,0:T(8,128)(2,1)S(1)}, u32[]{:S(2)}, u32[]{:S(2)}) collective-permute-start(bf16[512,256]{1,0:T(8,128)(2,1)S(1)} %get-tuple-element.18), channel_id=1, source_target_pairs={{0,24},{8,0},{16,8},{24,16},{1,25},{9,1},{17,9},{25,17},{2,26},{10... | collective-permute-start | bytes 786440 | tf_op jit(solution)/shard_map/ppermute | solution.py:23
  14.7 1.2 collective-permute-start.9
  15.9 0.7 collective-permute-done.15
  16.6 2.2 %collective-permute-start.10 = (bf16[512,256]{1,0:T(8,128)(2,1)S(1)}, bf16[512,256]{1,0:T(8,128)(2,1)S(1)}, u32[]{:S(2)}, u32[]{:S(2)}) collective-permute-start(bf16[512,256]{1,0:T(8,128)(2,1)S(1)} %get-tuple-element.17), channel_id=1, source_target_pairs={{0,6},{2,0},{4,2},{6,4},{1,7},{3,1},{5,3},{7,5},{8,14},{10,8},{12,... | collective-permute-start | bytes 786440 | tf_op jit(solution)/shard_map/ppermute | solution.py:23
  18.8 4.9 %collective-permute-done.1.refs_1_ = bf16[4,256,256]{2,1,0:T(8,128)(2,1)S(1)} collective-permute-done((bf16[4,256,256]{2,1,0:T(8,128)(2,1)S(1)}, bf16[4,256,256]{2,1,0:T(8,128)(2,1)S(1)}, u32[]{:S(2)}, u32[]{:S(2)}) %collective-permute-start.1) | collective-permute-done | bytes 524320 | tf_op jit(solution)/shard_map/ppermute | solution.py:23
  23.8 1.4 %collective-permute-start.17 = (bf16[256,256]{1,0:T(8,128)(2,1)S(1)}, bf16[256,256]{1,0:T(8,128)(2,1)S(1)}, u32[]{:S(2)}, u32[]{:S(2)}) collective-permute-start(bf16[256,256]{1,0:T(8,128)(2,1)S(1)} %slice.44), channel_id=1, source_target_pairs={{0,8},{8,16},{16,24},{24,0},{1,9},{9,17},{17,25},{25,1},{2,10},{10... | collective-permute-start | bytes 393224 | tf_op jit(solution)/shard_map/ppermute | solution.py:23
  25.2 1.5 %collective-permute-start.18 = (bf16[256,256]{1,0:T(8,128)(2,1)S(1)}, bf16[256,256]{1,0:T(8,128)(2,1)S(1)}, u32[]{:S(2)}, u32[]{:S(2)}) collective-permute-start(bf16[256,256]{1,0:T(8,128)(2,1)S(1)} %slice.45), channel_id=1, source_target_pairs={{0,24},{8,0},{16,8},{24,16},{1,25},{9,1},{17,9},{25,17},{2,26},{10... | collective-permute-start | bytes 393224 | tf_op jit(solution)/shard_map/ppermute | solution.py:23
  26.8 0.0 collective-permute-done.10
  26.8 1.3 %collective-permute-start.11 = (bf16[256,256]{1,0:T(8,128)(2,1)S(1)}, bf16[256,256]{1,0:T(8,128)(2,1)S(1)}, u32[]{:S(2)}, u32[]{:S(2)}) collective-permute-start(bf16[256,256]{1,0:T(8,128)(2,1)S(1)} %slice.42), channel_id=1, source_target_pairs={{0,2},{2,4},{4,6},{6,0},{1,3},{3,5},{5,7},{7,1},{8,10},{10,12},{12... | collective-permute-start | bytes 393224 | tf_op jit(solution)/shard_map/ppermute | solution.py:23
  28.1 2.7 %collective-permute-start.5 = (bf16[4,256,256]{2,1,0:T(8,128)(2,1)S(1)}, bf16[4,256,256]{2,1,0:T(8,128)(2,1)S(1)}, u32[]{:S(2)}, u32[]{:S(2)}) collective-permute-start(bf16[4,256,256]{2,1,0:T(8,128)(2,1)S(1)} %collective-permute-done.4.refs_4_), channel_id=1, source_target_pairs={{0,224},{32,0},{64,32},{96,64},{128,96},{160,128},{192,160},{224,1... | collective-permute-start | bytes 1572872 | tf_op jit(solution)/shard_map/ppermute | solution.py:23
  30.8 1.5 %collective-permute-start.12 = (bf16[256,256]{1,0:T(8,128)(2,1)S(1)}, bf16[256,256]{1,0:T(8,128)(2,1)S(1)}, u32[]{:S(2)}, u32[]{:S(2)}) collective-permute-start(bf16[256,256]{1,0:T(8,128)(2,1)S(1)} %slice.43), channel_id=1, source_target_pairs={{0,6},{2,0},{4,2},{6,4},{1,7},{3,1},{5,3},{7,5},{8,14},{10,8},{12,... | collective-permute-start | bytes 393224 | tf_op jit(solution)/shard_map/ppermute | solution.py:23
  32.4 5.1 %collective-permute-done.2.refs_2_ = bf16[4,256,256]{2,1,0:T(8,128)(2,1)S(1)} collective-permute-done((bf16[4,256,256]{2,1,0:T(8,128)(2,1)S(1)}, bf16[4,256,256]{2,1,0:T(8,128)(2,1)S(1)}, u32[]{:S(2)}, u32[]{:S(2)}) %collective-permute-start.2) | collective-permute-done | bytes 524320 | tf_op jit(solution)/shard_map/ppermute | solution.py:23
  37.6 1.3 %collective-permute-start.19 = (bf16[2048,256]{1,0:T(8,128)(2,1)S(1)}, bf16[2048,256]{1,0:T(8,128)(2,1)S(1)}, u32[]{:S(2)}, u32[]{:S(2)}) collective-permute-start(bf16[2048,256]{1,0:T(8,128)(2,1)S(1)} %constant_dynamic-update-slice_fusion.7.refs_12_), channel_id=1, source_target_pairs={{0,2},{2,4},{4,6},{6,0},{1,3},{3,5},{5,7},{7,1},{8,10},{10,12},{12... | collective-permute-start | bytes 3145736 | tf_op jit(solution)/shard_map/ppermute | solution.py:23
  38.9 1.5 %collective-permute-start.20 = (bf16[2048,256]{1,0:T(8,128)(2,1)S(1)}, bf16[2048,256]{1,0:T(8,128)(2,1)S(1)}, u32[]{:S(2)}, u32[]{:S(2)}) collective-permute-start(bf16[2048,256]{1,0:T(8,128)(2,1)S(1)} %constant_dynamic-update-slice_fusion.7.refs_12_), channel_id=1, source_target_pairs={{0,6},{2,0},{4,2},{6,4},{1,7},{3,1},{5,3},{7,5},{8,14},{10,8},{12,... | collective-permute-start | bytes 3145736 | tf_op jit(solution)/shard_map/ppermute | solution.py:23
  40.4 0.0 copy-start.7
  40.5 1.4 %collective-permute-start.13 = (bf16[2048,256]{1,0:T(8,128)(2,1)S(1)}, bf16[2048,256]{1,0:T(8,128)(2,1)S(1)}, u32[]{:S(2)}, u32[]{:S(2)}) collective-permute-start(bf16[2048,256]{1,0:T(8,128)(2,1)S(1)} %constant_dynamic-update-slice_fusion.2.refs_9_), channel_id=1, source_target_pairs={{0,8},{8,16},{16,24},{24,0},{1,9},{9,17},{17,25},{25,1},{2,10},{10... | collective-permute-start | bytes 3145736 | tf_op jit(solution)/shard_map/ppermute | solution.py:23
  41.8 1.5 %collective-permute-start.14 = (bf16[2048,256]{1,0:T(8,128)(2,1)S(1)}, bf16[2048,256]{1,0:T(8,128)(2,1)S(1)}, u32[]{:S(2)}, u32[]{:S(2)}) collective-permute-start(bf16[2048,256]{1,0:T(8,128)(2,1)S(1)} %constant_dynamic-update-slice_fusion.2.refs_9_), channel_id=1, source_target_pairs={{0,24},{8,0},{16,8},{24,16},{1,25},{9,1},{17,9},{25,17},{2,26},{10... | collective-permute-start | bytes 3145736 | tf_op jit(solution)/shard_map/ppermute | solution.py:23
  43.4 7.0 %collective-permute-done.3.refs_3_ = bf16[4,256,256]{2,1,0:T(8,128)(2,1)S(1)} collective-permute-done((bf16[4,256,256]{2,1,0:T(8,128)(2,1)S(1)}, bf16[4,256,256]{2,1,0:T(8,128)(2,1)S(1)}, u32[]{:S(2)}, u32[]{:S(2)}) %collective-permute-start.3) | collective-permute-done | bytes 524320 | tf_op jit(solution)/shard_map/ppermute | solution.py:23
  50.4 10.7 %collective-permute-done.6.refs_6_ = bf16[4,256,256]{2,1,0:T(8,128)(2,1)S(1)} collective-permute-done((bf16[4,256,256]{2,1,0:T(8,128)(2,1)S(1)}, bf16[4,256,256]{2,1,0:T(8,128)(2,1)S(1)}, u32[]{:S(2)}, u32[]{:S(2)}) %collective-permute-start.6) | collective-permute-done | bytes 524320 | tf_op jit(solution)/shard_map/ppermute | solution.py:23
  61.1 0.6 collective-permute-done.19.refs_13_
  61.7 2.4 %collective-permute-start.8 = (bf16[2,256,256]{2,1,0:T(8,128)(2,1)S(1)}, bf16[2,256,256]{2,1,0:T(8,128)(2,1)S(1)}, u32[]{:S(2)}, u32[]{:S(2)}) collective-permute-start(bf16[2,256,256]{2,1,0:T(8,128)(2,1)S(1)} %slice.41), channel_id=1, source_target_pairs={{0,224},{32,0},{64,32},{96,64},{128,96},{160,128},{192,160},{224,1... | collective-permute-start | bytes 786440 | tf_op jit(solution)/shard_map/ppermute | solution.py:23
  64.2 1.1 collective-permute-start.23
  65.3 1.8 %collective-permute-start.24 = (bf16[1024,256]{1,0:T(8,128)(2,1)S(1)}, bf16[1024,256]{1,0:T(8,128)(2,1)S(1)}, u32[]{:S(2)}, u32[]{:S(2)}) collective-permute-start(bf16[1024,256]{1,0:T(8,128)(2,1)S(1)} %slice.49), channel_id=1, source_target_pairs={{0,6},{2,0},{4,2},{6,4},{1,7},{3,1},{5,3},{7,5},{8,14},{10,8},{12,... | collective-permute-start | bytes 1572872 | tf_op jit(solution)/shard_map/ppermute | solution.py:23
  67.2 1.4 %collective-permute-start.21 = (bf16[1024,256]{1,0:T(8,128)(2,1)S(1)}, bf16[1024,256]{1,0:T(8,128)(2,1)S(1)}, u32[]{:S(2)}, u32[]{:S(2)}) collective-permute-start(bf16[1024,256]{1,0:T(8,128)(2,1)S(1)} %slice.46), channel_id=1, source_target_pairs={{0,8},{8,16},{16,24},{24,0},{1,9},{9,17},{17,25},{25,1},{2,10},{10... | collective-permute-start | bytes 1572872 | tf_op jit(solution)/shard_map/ppermute | solution.py:23
  68.6 1.7 %collective-permute-start.22 = (bf16[1024,256]{1,0:T(8,128)(2,1)S(1)}, bf16[1024,256]{1,0:T(8,128)(2,1)S(1)}, u32[]{:S(2)}, u32[]{:S(2)}) collective-permute-start(bf16[1024,256]{1,0:T(8,128)(2,1)S(1)} %slice.47), channel_id=1, source_target_pairs={{0,24},{8,0},{16,8},{24,16},{1,25},{9,1},{17,9},{25,17},{2,26},{10... | collective-permute-start | bytes 1572872 | tf_op jit(solution)/shard_map/ppermute | solution.py:23
  70.3 10.1 %near.1 = (f32[1024,256]{1,0:T(8,128)S(1)}, f32[1024,256]{1,0:T(8,128)}, bf16[1024,512]{1,0:T(8,128)(2,1)}, bf16[1024,512]{1,0:T(8,128)(2,1)}) custom-call(s32[4]{0:T(128)S(1)} %pad_add_fusion.pos, bf16[4,256,256]{2,1,0:T(8,128)(2,1)S(1)} %constant_dynamic-update-slice_fusion.refs_0_, bf16[4,256,256]{2,1,0:T(8,128)(2,1)S(1)} %collective-permute-done.1.refs_1_, ...), custom_call_target="tpu_custom_call" | custom-call | flops 3200000000 | bytes 12000000 | tf_op jit(solution)/shard_map/near/pallas_call | solution.py:187
  80.4 1.2 copy-done
  81.6 3.9 %far.1 = (f32[1024,256]{1,0:T(8,128)S(1)}, f32[1024,256]{1,0:T(8,128)}) custom-call(bf16[1024,512]{1,0:T(8,128)(2,1)S(1)} %copy-done, bf16[1024,512]{1,0:T(8,128)(2,1)} %get-tuple-element.20.bx, bf16[1024,256]{1,0:T(8,128)(2,1)S(1)} %collective-permute-done.21.q_top0, ...), custom_call_target="tpu_custom_call", output_to_operand_aliasing={{0}: (6, {}), {1}: (7, {})} | custom-call | flops 1100000000 | bytes 4000000 | tf_op jit(solution)/shard_map/far/pallas_call | solution.py:205
  85.5 5.1 %collective-permute-start.25 = (f32[1024,256]{1,0:T(8,128)}, f32[1024,256]{1,0:T(8,128)S(1)}, u32[]{:S(2)}, u32[]{:S(2)}) collective-permute-start(f32[1024,256]{1,0:T(8,128)} %get-tuple-element.24), channel_id=1, source_target_pairs={{0,1},{1,0},{2,3},{3,2},{4,5},{5,4},{6,7},{7,6},{8,9},{9,8},{10,11... | collective-permute-start | bytes 3145736 | tf_op jit(solution)/shard_map/ppermute | solution.py:215
  90.5 0.1 copy.11.keep
  90.6 2.4 %collective-permute-done.25.recv = f32[1024,256]{1,0:T(8,128)S(1)} collective-permute-done((f32[1024,256]{1,0:T(8,128)}, f32[1024,256]{1,0:T(8,128)S(1)}, u32[]{:S(2)}, u32[]{:S(2)}) %collective-permute-start.25) | collective-permute-done | bytes 1048608 | tf_op jit(solution)/shard_map/ppermute | solution.py:215
  93.0 0.7 copy-done.2
  93.7 1.9 %final.1 = (f32[1024,256]{1,0:T(8,128)}, f32[8,128]{1,0:T(8,128)S(1)}) custom-call(s32[4]{0:T(128)S(1)} %pad_add_fusion.pos, s32[8,2]{1,0:T(8,128)S(1)} %copy.11.keep, s32[8]{0:T(128)S(1)} %copy-done.2, f32[1024,256]{1,0:T(8,128)S(1)} %get-tuple-element.23.own, f32[1024,256]{1,0:T(8,128)S(1)} %collective-permute-done.25.recv, ...), custom_call_target="tpu_custom_call" | custom-call | tf_op jit(solution)/shard_map/final/pallas_call | solution.py:216
  95.6 10.9 %all_to_all.10 = f32[16,8,128]{2,1,0:T(8,128)S(1)} all-to-all(f32[16,8,128]{2,1,0:T(8,128)S(1)} %broadcast_in_dim.4), channel_id=1, replica_groups=mesh['row'=8,'col_0'=4,'col_1'=4,'layer'=2] {'col_0','col_1'}, dimensions={0} | all-to-all | bytes 131072 | tf_op jit(solution)/shard_map/all_to_all | solution.py:165
  106.6 11.4 %all_to_all.11 = f32[8,8,128]{2,1,0:T(8,128)S(1)} all-to-all(f32[8,8,128]{2,1,0:T(8,128)S(1)} %broadcast_in_dim.5), channel_id=1, replica_groups=mesh['row'=8,'col_0'=4,'col_1'=4,'layer'=2] {'row'}, dimensions={0} | all-to-all | bytes 65536 | tf_op jit(solution)/shard_map/all_to_all | solution.py:165
  118.0 3.2 %collective-permute-start.26 = (f32[8,128]{1,0:T(8,128)S(1)}, f32[8,128]{1,0:T(8,128)S(1)}, u32[]{:S(2)}, u32[]{:S(2)}) collective-permute-start(f32[8,128]{1,0:T(8,128)S(1)} %reduce_sum.28), channel_id=1, source_target_pairs={{0,1},{1,0},{2,3},{3,2},{4,5},{5,4},{6,7},{7,6},{8,9},{9,8},{10,11... | collective-permute-start | bytes 12296 | tf_op jit(solution)/shard_map/ppermute | solution.py:166
  121.2 0.8 collective-permute-done.26
  122.0 0.6 add_reduce_fusion
  (63 shorter events, 0.5 us)
Async XLA Ops:
  0.6 0.7 copy-start.9
  1.5 1.0 copy-start.1
  3.3 4.5 %collective-permute-start = (bf16[2,256,256]{2,1,0:T(8,128)(2,1)S(1)}, bf16[2,256,256]{2,1,0:T(8,128)(2,1)S(1)}, u32[]{:S(2)}, u32[]{:S(2)}) collective-permute-start(bf16[2,256,256]{2,1,0:T(8,128)(2,1)S(1)} %get-tuple-element.16), channel_id=1, source_target_pairs={{0,1},{1,0},{2,3},{3,2},{4,5},{5,4},{6,7},{7,6},{8,9},{9,8},{10,11... | collective-permute-start | bytes 786440 | tf_op jit(solution)/shard_map/ppermute | solution.py:180
  7.9 15.9 %collective-permute-start.1 = (bf16[4,256,256]{2,1,0:T(8,128)(2,1)S(1)}, bf16[4,256,256]{2,1,0:T(8,128)(2,1)S(1)}, u32[]{:S(2)}, u32[]{:S(2)}) collective-permute-start(bf16[4,256,256]{2,1,0:T(8,128)(2,1)S(1)} %constant_dynamic-update-slice_fusion.refs_0_), channel_id=1, source_target_pairs={{0,32},{32,64},{64,96},{96,128},{128,160},{160,192},{192,224},{224... | collective-permute-start | bytes 1572872 | tf_op jit(solution)/shard_map/ppermute | solution.py:23
  7.9 8.7 %collective-permute-start.15 = (bf16[512,256]{1,0:T(8,128)(2,1)S(1)}, bf16[512,256]{1,0:T(8,128)(2,1)S(1)}, u32[]{:S(2)}, u32[]{:S(2)}) collective-permute-start(bf16[512,256]{1,0:T(8,128)(2,1)S(1)} %get-tuple-element.18), channel_id=1, source_target_pairs={{0,8},{8,16},{16,24},{24,0},{1,9},{9,17},{17,25},{25,1},{2,10},{10... | collective-permute-start | bytes 786440 | tf_op jit(solution)/shard_map/ppermute | solution.py:23
  9.1 19.0 %collective-permute-start.4 = (bf16[4,256,256]{2,1,0:T(8,128)(2,1)S(1)}, bf16[4,256,256]{2,1,0:T(8,128)(2,1)S(1)}, u32[]{:S(2)}, u32[]{:S(2)}) collective-permute-start(bf16[4,256,256]{2,1,0:T(8,128)(2,1)S(1)} %constant_dynamic-update-slice_fusion.refs_0_), channel_id=1, source_target_pairs={{0,224},{32,0},{64,32},{96,64},{128,96},{160,128},{192,160},{224,1... | collective-permute-start | bytes 1572872 | tf_op jit(solution)/shard_map/ppermute | solution.py:23
  13.2 10.7 %collective-permute-start.16 = (bf16[512,256]{1,0:T(8,128)(2,1)S(1)}, bf16[512,256]{1,0:T(8,128)(2,1)S(1)}, u32[]{:S(2)}, u32[]{:S(2)}) collective-permute-start(bf16[512,256]{1,0:T(8,128)(2,1)S(1)} %get-tuple-element.18), channel_id=1, source_target_pairs={{0,24},{8,0},{16,8},{24,16},{1,25},{9,1},{17,9},{25,17},{2,26},{10... | collective-permute-start | bytes 786440 | tf_op jit(solution)/shard_map/ppermute | solution.py:23
  14.7 10.6 %collective-permute-start.9 = (bf16[512,256]{1,0:T(8,128)(2,1)S(1)}, bf16[512,256]{1,0:T(8,128)(2,1)S(1)}, u32[]{:S(2)}, u32[]{:S(2)}) collective-permute-start(bf16[512,256]{1,0:T(8,128)(2,1)S(1)} %get-tuple-element.17), channel_id=1, source_target_pairs={{0,2},{2,4},{4,6},{6,0},{1,3},{3,5},{5,7},{7,1},{8,10},{10,12},{12... | collective-permute-start | bytes 786440 | tf_op jit(solution)/shard_map/ppermute | solution.py:23
  16.6 10.2 %collective-permute-start.10 = (bf16[512,256]{1,0:T(8,128)(2,1)S(1)}, bf16[512,256]{1,0:T(8,128)(2,1)S(1)}, u32[]{:S(2)}, u32[]{:S(2)}) collective-permute-start(bf16[512,256]{1,0:T(8,128)(2,1)S(1)} %get-tuple-element.17), channel_id=1, source_target_pairs={{0,6},{2,0},{4,2},{6,4},{1,7},{3,1},{5,3},{7,5},{8,14},{10,8},{12,... | collective-permute-start | bytes 786440 | tf_op jit(solution)/shard_map/ppermute | solution.py:23
  23.8 13.8 %collective-permute-start.2 = (bf16[4,256,256]{2,1,0:T(8,128)(2,1)S(1)}, bf16[4,256,256]{2,1,0:T(8,128)(2,1)S(1)}, u32[]{:S(2)}, u32[]{:S(2)}) collective-permute-start(bf16[4,256,256]{2,1,0:T(8,128)(2,1)S(1)} %collective-permute-done.1.refs_1_), channel_id=1, source_target_pairs={{0,32},{32,64},{64,96},{96,128},{128,160},{160,192},{192,224},{224... | collective-permute-start | bytes 1572872 | tf_op jit(solution)/shard_map/ppermute | solution.py:23
  23.8 7.0 %collective-permute-start.17 = (bf16[256,256]{1,0:T(8,128)(2,1)S(1)}, bf16[256,256]{1,0:T(8,128)(2,1)S(1)}, u32[]{:S(2)}, u32[]{:S(2)}) collective-permute-start(bf16[256,256]{1,0:T(8,128)(2,1)S(1)} %slice.44), channel_id=1, source_target_pairs={{0,8},{8,16},{16,24},{24,0},{1,9},{9,17},{17,25},{25,1},{2,10},{10... | collective-permute-start | bytes 393224 | tf_op jit(solution)/shard_map/ppermute | solution.py:23
  25.2 12.3 %collective-permute-start.18 = (bf16[256,256]{1,0:T(8,128)(2,1)S(1)}, bf16[256,256]{1,0:T(8,128)(2,1)S(1)}, u32[]{:S(2)}, u32[]{:S(2)}) collective-permute-start(bf16[256,256]{1,0:T(8,128)(2,1)S(1)} %slice.45), channel_id=1, source_target_pairs={{0,24},{8,0},{16,8},{24,16},{1,25},{9,1},{17,9},{25,17},{2,26},{10... | collective-permute-start | bytes 393224 | tf_op jit(solution)/shard_map/ppermute | solution.py:23
  26.8 12.0 %collective-permute-start.11 = (bf16[256,256]{1,0:T(8,128)(2,1)S(1)}, bf16[256,256]{1,0:T(8,128)(2,1)S(1)}, u32[]{:S(2)}, u32[]{:S(2)}) collective-permute-start(bf16[256,256]{1,0:T(8,128)(2,1)S(1)} %slice.42), channel_id=1, source_target_pairs={{0,2},{2,4},{4,6},{6,0},{1,3},{3,5},{5,7},{7,1},{8,10},{10,12},{12... | collective-permute-start | bytes 393224 | tf_op jit(solution)/shard_map/ppermute | solution.py:23
  28.1 13.7 %collective-permute-start.5 = (bf16[4,256,256]{2,1,0:T(8,128)(2,1)S(1)}, bf16[4,256,256]{2,1,0:T(8,128)(2,1)S(1)}, u32[]{:S(2)}, u32[]{:S(2)}) collective-permute-start(bf16[4,256,256]{2,1,0:T(8,128)(2,1)S(1)} %collective-permute-done.4.refs_4_), channel_id=1, source_target_pairs={{0,224},{32,0},{64,32},{96,64},{128,96},{160,128},{192,160},{224,1... | collective-permute-start | bytes 1572872 | tf_op jit(solution)/shard_map/ppermute | solution.py:23
  30.8 9.6 %collective-permute-start.12 = (bf16[256,256]{1,0:T(8,128)(2,1)S(1)}, bf16[256,256]{1,0:T(8,128)(2,1)S(1)}, u32[]{:S(2)}, u32[]{:S(2)}) collective-permute-start(bf16[256,256]{1,0:T(8,128)(2,1)S(1)} %slice.43), channel_id=1, source_target_pairs={{0,6},{2,0},{4,2},{6,4},{1,7},{3,1},{5,3},{7,5},{8,14},{10,8},{12,... | collective-permute-start | bytes 393224 | tf_op jit(solution)/shard_map/ppermute | solution.py:23
  37.5 12.8 %collective-permute-start.3 = (bf16[4,256,256]{2,1,0:T(8,128)(2,1)S(1)}, bf16[4,256,256]{2,1,0:T(8,128)(2,1)S(1)}, u32[]{:S(2)}, u32[]{:S(2)}) collective-permute-start(bf16[4,256,256]{2,1,0:T(8,128)(2,1)S(1)} %collective-permute-done.2.refs_2_), channel_id=1, source_target_pairs={{0,32},{32,64},{64,96},{96,128},{128,160},{160,192},{192,224},{224... | collective-permute-start | bytes 1572872 | tf_op jit(solution)/shard_map/ppermute | solution.py:23
  37.6 26.6 %copy-start.8 = (bf16[2048,256]{1,0:T(8,128)(2,1)}, bf16[2048,256]{1,0:T(8,128)(2,1)S(1)}, u32[]{:S(2)}) copy-start(bf16[2048,256]{1,0:T(8,128)(2,1)S(1)} %constant_dynamic-update-slice_fusion.7.refs_12_) | copy-start | bytes 3145732
  37.6 24.2 %collective-permute-start.19 = (bf16[2048,256]{1,0:T(8,128)(2,1)S(1)}, bf16[2048,256]{1,0:T(8,128)(2,1)S(1)}, u32[]{:S(2)}, u32[]{:S(2)}) collective-permute-start(bf16[2048,256]{1,0:T(8,128)(2,1)S(1)} %constant_dynamic-update-slice_fusion.7.refs_12_), channel_id=1, source_target_pairs={{0,2},{2,4},{4,6},{6,0},{1,3},{3,5},{5,7},{7,1},{8,10},{10,12},{12... | collective-permute-start | bytes 3145736 | tf_op jit(solution)/shard_map/ppermute | solution.py:23
  38.9 25.3 %collective-permute-start.20 = (bf16[2048,256]{1,0:T(8,128)(2,1)S(1)}, bf16[2048,256]{1,0:T(8,128)(2,1)S(1)}, u32[]{:S(2)}, u32[]{:S(2)}) collective-permute-start(bf16[2048,256]{1,0:T(8,128)(2,1)S(1)} %constant_dynamic-update-slice_fusion.7.refs_12_), channel_id=1, source_target_pairs={{0,6},{2,0},{4,2},{6,4},{1,7},{3,1},{5,3},{7,5},{8,14},{10,8},{12,... | collective-permute-start | bytes 3145736 | tf_op jit(solution)/shard_map/ppermute | solution.py:23
  40.4 29.8 %copy-start.7 = (bf16[2048,256]{1,0:T(8,128)(2,1)}, bf16[2048,256]{1,0:T(8,128)(2,1)S(1)}, u32[]{:S(2)}) copy-start(bf16[2048,256]{1,0:T(8,128)(2,1)S(1)} %constant_dynamic-update-slice_fusion.2.refs_9_) | copy-start | bytes 3145732
  40.5 24.8 %collective-permute-start.13 = (bf16[2048,256]{1,0:T(8,128)(2,1)S(1)}, bf16[2048,256]{1,0:T(8,128)(2,1)S(1)}, u32[]{:S(2)}, u32[]{:S(2)}) collective-permute-start(bf16[2048,256]{1,0:T(8,128)(2,1)S(1)} %constant_dynamic-update-slice_fusion.2.refs_9_), channel_id=1, source_target_pairs={{0,8},{8,16},{16,24},{24,0},{1,9},{9,17},{17,25},{25,1},{2,10},{10... | collective-permute-start | bytes 3145736 | tf_op jit(solution)/shard_map/ppermute | solution.py:23
  41.8 25.3 %collective-permute-start.14 = (bf16[2048,256]{1,0:T(8,128)(2,1)S(1)}, bf16[2048,256]{1,0:T(8,128)(2,1)S(1)}, u32[]{:S(2)}, u32[]{:S(2)}) collective-permute-start(bf16[2048,256]{1,0:T(8,128)(2,1)S(1)} %constant_dynamic-update-slice_fusion.2.refs_9_), channel_id=1, source_target_pairs={{0,24},{8,0},{16,8},{24,16},{1,25},{9,1},{17,9},{25,17},{2,26},{10... | collective-permute-start | bytes 3145736 | tf_op jit(solution)/shard_map/ppermute | solution.py:23
  50.4 10.7 %collective-permute-start.6 = (bf16[4,256,256]{2,1,0:T(8,128)(2,1)S(1)}, bf16[4,256,256]{2,1,0:T(8,128)(2,1)S(1)}, u32[]{:S(2)}, u32[]{:S(2)}) collective-permute-start(bf16[4,256,256]{2,1,0:T(8,128)(2,1)S(1)} %collective-permute-done.5.refs_5_), channel_id=1, source_target_pairs={{0,224},{32,0},{64,32},{96,64},{128,96},{160,128},{192,160},{224,1... | collective-permute-start | bytes 1572872 | tf_op jit(solution)/shard_map/ppermute | solution.py:23
  61.1 7.5 %collective-permute-start.7 = (bf16[2,256,256]{2,1,0:T(8,128)(2,1)S(1)}, bf16[2,256,256]{2,1,0:T(8,128)(2,1)S(1)}, u32[]{:S(2)}, u32[]{:S(2)}) collective-permute-start(bf16[2,256,256]{2,1,0:T(8,128)(2,1)S(1)} %slice.40), channel_id=1, source_target_pairs={{0,32},{32,64},{64,96},{96,128},{128,160},{160,192},{192,224},{224... | collective-permute-start | bytes 786440 | tf_op jit(solution)/shard_map/ppermute | solution.py:23
  61.7 3.6 %copy-start.3 = (bf16[2048,256]{1,0:T(8,128)(2,1)}, bf16[2048,256]{1,0:T(8,128)(2,1)S(1)}, u32[]{:S(2)}) copy-start(bf16[2048,256]{1,0:T(8,128)(2,1)S(1)} %collective-permute-done.19.refs_13_) | copy-start | bytes 3145732
  61.7 8.5 %collective-permute-start.8 = (bf16[2,256,256]{2,1,0:T(8,128)(2,1)S(1)}, bf16[2,256,256]{2,1,0:T(8,128)(2,1)S(1)}, u32[]{:S(2)}, u32[]{:S(2)}) collective-permute-start(bf16[2,256,256]{2,1,0:T(8,128)(2,1)S(1)} %slice.41), channel_id=1, source_target_pairs={{0,224},{32,0},{64,32},{96,64},{128,96},{160,128},{192,160},{224,1... | collective-permute-start | bytes 786440 | tf_op jit(solution)/shard_map/ppermute | solution.py:23
  64.2 3.0 %copy-start.4 = (bf16[2048,256]{1,0:T(8,128)(2,1)}, bf16[2048,256]{1,0:T(8,128)(2,1)S(1)}, u32[]{:S(2)}) copy-start(bf16[2048,256]{1,0:T(8,128)(2,1)S(1)} %collective-permute-done.20.refs_14_) | copy-start | bytes 3145732
  64.2 16.1 %collective-permute-start.23 = (bf16[1024,256]{1,0:T(8,128)(2,1)S(1)}, bf16[1024,256]{1,0:T(8,128)(2,1)S(1)}, u32[]{:S(2)}, u32[]{:S(2)}) collective-permute-start(bf16[1024,256]{1,0:T(8,128)(2,1)S(1)} %slice.48), channel_id=1, source_target_pairs={{0,2},{2,4},{4,6},{6,0},{1,3},{3,5},{5,7},{7,1},{8,10},{10,12},{12... | collective-permute-start | bytes 1572872 | tf_op jit(solution)/shard_map/ppermute | solution.py:23
  65.3 3.3 %copy-start.5 = (bf16[2048,256]{1,0:T(8,128)(2,1)}, bf16[2048,256]{1,0:T(8,128)(2,1)S(1)}, u32[]{:S(2)}) copy-start(bf16[2048,256]{1,0:T(8,128)(2,1)S(1)} %collective-permute-done.13.refs_10_) | copy-start | bytes 3145732
  65.3 15.0 %collective-permute-start.24 = (bf16[1024,256]{1,0:T(8,128)(2,1)S(1)}, bf16[1024,256]{1,0:T(8,128)(2,1)S(1)}, u32[]{:S(2)}, u32[]{:S(2)}) collective-permute-start(bf16[1024,256]{1,0:T(8,128)(2,1)S(1)} %slice.49), channel_id=1, source_target_pairs={{0,6},{2,0},{4,2},{6,4},{1,7},{3,1},{5,3},{7,5},{8,14},{10,8},{12,... | collective-permute-start | bytes 1572872 | tf_op jit(solution)/shard_map/ppermute | solution.py:23
  67.1 3.1 %copy-start.6 = (bf16[2048,256]{1,0:T(8,128)(2,1)}, bf16[2048,256]{1,0:T(8,128)(2,1)S(1)}, u32[]{:S(2)}) copy-start(bf16[2048,256]{1,0:T(8,128)(2,1)S(1)} %collective-permute-done.14.refs_11_) | copy-start | bytes 3145732
  67.2 13.2 %collective-permute-start.21 = (bf16[1024,256]{1,0:T(8,128)(2,1)S(1)}, bf16[1024,256]{1,0:T(8,128)(2,1)S(1)}, u32[]{:S(2)}, u32[]{:S(2)}) collective-permute-start(bf16[1024,256]{1,0:T(8,128)(2,1)S(1)} %slice.46), channel_id=1, source_target_pairs={{0,8},{8,16},{16,24},{24,0},{1,9},{9,17},{17,25},{25,1},{2,10},{10... | collective-permute-start | bytes 1572872 | tf_op jit(solution)/shard_map/ppermute | solution.py:23
  68.6 11.8 %collective-permute-start.22 = (bf16[1024,256]{1,0:T(8,128)(2,1)S(1)}, bf16[1024,256]{1,0:T(8,128)(2,1)S(1)}, u32[]{:S(2)}, u32[]{:S(2)}) collective-permute-start(bf16[1024,256]{1,0:T(8,128)(2,1)S(1)} %slice.47), channel_id=1, source_target_pairs={{0,24},{8,0},{16,8},{24,16},{1,25},{9,1},{17,9},{25,17},{2,26},{10... | collective-permute-start | bytes 1572872 | tf_op jit(solution)/shard_map/ppermute | solution.py:23
  80.4 1.2 copy-start
  85.5 5.1 %copy-start.10 = (s32[8,2]{0,1:T(2,128)S(1)}, s32[8,2]{0,1:T(2,128)}, u32[]{:S(2)}) copy-start(s32[8,2]{0,1:T(2,128)} %param.6) | copy-start | bytes 196
  85.5 7.6 %collective-permute-start.25 = (f32[1024,256]{1,0:T(8,128)}, f32[1024,256]{1,0:T(8,128)S(1)}, u32[]{:S(2)}, u32[]{:S(2)}) collective-permute-start(f32[1024,256]{1,0:T(8,128)} %get-tuple-element.24), channel_id=1, source_target_pairs={{0,1},{1,0},{2,3},{3,2},{4,5},{5,4},{6,7},{7,6},{8,9},{9,8},{10,11... | collective-permute-start | bytes 3145736 | tf_op jit(solution)/shard_map/ppermute | solution.py:215
  93.0 0.7 copy-start.2
  118.0 4.1 %collective-permute-start.26 = (f32[8,128]{1,0:T(8,128)S(1)}, f32[8,128]{1,0:T(8,128)S(1)}, u32[]{:S(2)}, u32[]{:S(2)}) collective-permute-start(f32[8,128]{1,0:T(8,128)S(1)} %reduce_sum.28), channel_id=1, source_target_pairs={{0,1},{1,0},{2,3},{3,2},{4,5},{5,4},{6,7},{7,6},{8,9},{9,8},{10,11... | collective-permute-start | bytes 12296 | tf_op jit(solution)/shard_map/ppermute | solution.py:166

commit v2 on v1

v2 whole, which is shorter than its diff:
```python
import functools

import jax
import jax.numpy as jnp
from jax import lax
from jax.experimental import pallas as pl
from jax.experimental.pallas import tpu as pltpu
from jax.sharding import Mesh
from jax.sharding import PartitionSpec as P

BLK = 128
Y, X = "col_0", "col_1"
COL_LAYER = (Y, X, "layer")
SMEM = pl.BlockSpec(memory_space=pltpu.SMEM)
VMEM = pl.BlockSpec(memory_space=pltpu.VMEM)
HBM = pl.BlockSpec(memory_space=pl.ANY)


def room(mib):
    return pltpu.CompilerParams(vmem_limit_bytes=mib * 1024 * 1024)


def shift(value, axis, off):
    n = lax.axis_size(axis)
    return lax.ppermute(value, axis, [(i, (i + off) % n) for i in range(n)])


def turn(value, stage, off):
    nz, ny, nx = (lax.axis_size(a) for a in ("row", Y, X))
    at = lambda z, y, x, core: ((z * ny + y) * nx + x) * 2 + core
    pairs = []
    for z in range(nz):
        for y in range(ny):
            for x in range(nx):
                for core in range(2):
                    along_x = core == stage
                    to = (y, (x + off) % nx) if along_x else ((y + off) % ny, x)
                    pairs.append((at(z, y, x, core), at(z, *to, core)))
    return lax.ppermute(value, ("row", Y, X, "layer"), pairs)


def keep_kernel(x, out):
    pass


def hold(value, us):
    return pl.pallas_call(
        keep_kernel,
        out_shape=jax.ShapeDtypeStruct(value.shape, value.dtype),
        in_specs=[HBM],
        out_specs=HBM,
        input_output_aliases={0: 0},
        compiler_params=room(1),
        name="hold",
        cost_estimate=pl.CostEstimate(flops=int(us * 1e9), bytes_accessed=0, transcendentals=0),
    )(value)


def ring4(own, stage):
    half = own.shape[0] // 2
    plus, minus = turn(own, stage, 1), turn(own, stage, -1)
    return plus, minus, turn(plus[:half], stage, 1), turn(minus[half:], stage, -1)


def ring8(own, axis):
    half = own.shape[0] // 2
    plus, minus = [own], [own]
    for _ in range(3):
        plus.append(hold(shift(plus[-1], axis, 1), 4.0))
        minus.append(hold(shift(minus[-1], axis, -1), 4.0))
    far = (shift(plus[-1][:half], axis, 1), shift(minus[-1][half:], axis, -1))
    return plus[1:], minus[1:], far


def mask_kernel(pos, bm, x, m, own, peer):
    layer = pos[3]
    rows = []
    for i in range(8):
        parts = [
            x[pl.ds(i * BLK, BLK), pl.ds(j * BLK, BLK)] * bm[j, i].astype(jnp.float32).astype(jnp.bfloat16)
            for j in range(2)
        ]
        rows.append(jnp.concatenate(parts, axis=1))
    for i in range(8):
        m[pl.ds(i * BLK, BLK), :] = rows[i]
        at, cls, inner = i // 4, (i // 2) % 2, i % 2

        @pl.when(layer == cls)
        def _():
            own[at, pl.ds(inner * BLK, BLK), :] = rows[i]

        @pl.when(layer != cls)
        def _():
            peer[at, pl.ds(inner * BLK, BLK), :] = rows[i]


def place(pos, d, half):
    r, y, x = pos[0], pos[1], pos[2]
    src = lax.rem(r - d + 8, 8)
    col = src * 2 + half
    dy, dx = lax.rem(col // 4 - y + 4, 4), lax.rem(lax.rem(col, 4) - x + 4, 4)
    rank = lambda o: jnp.where(o == 0, 0, jnp.where(o == 3, 1, jnp.where(o == 1, 2, 3)))
    return rank(dy), rank(dx)


def rows_kernel(pos, *refs):
    z_refs, b = refs[:9], refs[9]
    pieces = [(d, ch, rh, d, 2 * ch + rh) for d in range(4) for ch in range(2) for rh in range(2)]
    pieces += [(-d, ch, rh, 3 + d, 2 * ch + rh) for d in range(1, 4) for ch in range(2) for rh in range(2)]
    pieces += [(4, ch, rh, 7 + ch, rh) for ch in range(2) for rh in range(2)]
    for d, ch, rh, ref, at in pieces:
        ry, rx = place(pos, d, rh)
        to = jnp.where(pos[3] == 0, ry * 4 + rx, rx * 4 + ry)
        b[ch, pl.ds(pl.multiple_of(to * 256, 256), 256), :] = z_refs[ref][at]


def near_kernel(b, line, line_p, line_m, p_own, p_peer):
    @pl.loop(0, 4)
    def _(i):
        a = []
        for src in (line, line_p, line_m):
            for k in range(4):
                a.append(src[pl.ds(pl.multiple_of(k * 1024 + i * 256, 256), 256), :])
        rows = pl.ds(pl.multiple_of(i * 256, 256), 256)
        a = jnp.concatenate(a, axis=1)
        p_peer[rows, :] = jnp.dot(a, b[1, pl.ds(0, 3072), :], preferred_element_type=jnp.float32)
        p_own[rows, :] = jnp.dot(a, b[0, pl.ds(0, 3072), :], preferred_element_type=jnp.float32)


def far_rows(b, q0, q1, ch, old, new):
    for i in range(4):
        rows = pl.ds(i * 256, 256)
        a = jnp.concatenate([(q0, q1)[k // 2][pl.ds((k % 2) * 1024 + i * 256, 256), :] for k in range(4)], axis=1)
        new[rows, :] = old[rows, :] + jnp.dot(a, b[ch, pl.ds(3072, 1024), :], preferred_element_type=jnp.float32)


def far_own_kernel(b, q0, q1, p_own, tie, new):
    far_rows(b, q0, q1, 0, p_own, new)


def far_peer_kernel(pos, keep, flag, m, b, q0, q1, p_own, p_peer, new, out):
    lane = lax.broadcasted_iota(jnp.int32, (1, BLK), 1)
    eye = lax.broadcasted_iota(jnp.int32, (BLK, BLK), 0) == lax.broadcasted_iota(jnp.int32, (BLK, BLK), 1)
    chip, core = pos[1] * 4 + pos[2], pos[3]
    out[...] = jnp.zeros((1, BLK), jnp.float32)
    far_rows(b, q0, q1, 1, p_peer, new)

    def trace(block):
        line = jnp.sum(jnp.where(eye, block, 0.0), axis=0, keepdims=True)
        return jnp.sum(line, axis=1, keepdims=True)

    @pl.when(chip // 2 == pos[0])
    def _():
        total = jnp.zeros((1, BLK), jnp.float32)
        for ch in range(2):
            side = core if ch == 0 else 1 - core
            for j in range(2):
                i = (chip % 2) * 4 + side * 2 + j
                start = pl.multiple_of(i * BLK, BLK)
                rows, cols = pl.ds(start, BLK), pl.ds(j * BLK, BLK)
                if ch == 1:
                    block = new[rows, cols]
                else:
                    block = p_own[rows, cols]
                    for k in range(4):
                        a = (q0, q1)[k // 2][pl.ds(pl.multiple_of((k % 2) * 1024 + start, BLK), BLK), :]
                        block += jnp.dot(a, b[ch, pl.ds(3072 + k * 256, 256), cols], preferred_element_type=jnp.float32)
                total += jnp.where(lane == i, trace(block), 0.0)
                if ch == 0:
                    total += jnp.where(lane == 8 + i, keep[j, i].astype(jnp.float32), 0.0)
                    total += jnp.where(lane == 16 + i, trace(m[rows, cols].astype(jnp.float32)), 0.0)
                    total += jnp.where(lane == 24 + i, flag[i].astype(jnp.float32), 0.0)
        out[...] = total


def final_kernel(keep, flag, own, recv, m, out):
    for i in range(8):
        take = flag[i] == 1
        sign, twice = jnp.where(take, 1.0, -1.0), jnp.where(take, 0.0, 2.0)
        for j in range(2):
            at = (pl.ds(i * BLK, BLK), pl.ds(j * BLK, BLK))
            square = own[at] + recv[at]
            out[at] = (twice * m[at].astype(jnp.float32) + sign * square) * keep[j, i].astype(jnp.float32)


def bf16(*shape):
    return jax.ShapeDtypeStruct(shape, jnp.bfloat16)


def f32(*shape):
    return jax.ShapeDtypeStruct(shape, jnp.float32)


def trace_of(parts):
    spread = jnp.broadcast_to(parts[None], (128, 1, BLK))
    rows = lax.all_to_all(spread, ("row", Y, X), 0, 0).reshape(8, 16, BLK).sum(axis=1)
    rows = rows + lax.ppermute(rows, "layer", [(0, 1), (1, 0)])
    square, keep, linear, branch = (rows[:, 8 * n : 8 * n + 8] for n in range(4))
    return jnp.sum(keep * jnp.where(branch == 1.0, square, 2.0 * linear - square))


def on_device(density, block_mask, keep_mask, branch_flag):
    pos = jnp.stack([lax.axis_index(a) for a in ("row", Y, X, "layer")]).astype(jnp.int32)
    swap = [(0, 1), (1, 0)]
    m, own_rows, peer_rows = pl.pallas_call(
        mask_kernel,
        out_shape=[bf16(1024, 256), bf16(2, 256, 256), bf16(2, 256, 256)],
        in_specs=[SMEM, SMEM, VMEM],
        out_specs=[VMEM] * 3,
        compiler_params=room(6),
        name="mask",
    )(pos, block_mask.T, density)
    other = lax.ppermute(peer_rows, "layer", swap)
    z_tile = jnp.concatenate([own_rows, other], axis=0)
    z_plus, z_minus, z_far = ring8(z_tile, "row")
    line = jnp.concatenate([m, *ring4(m, 0)], axis=0)
    line_p, line_m, q0, q1 = ring4(line, 1)
    inner = pl.pallas_call(
        rows_kernel,
        out_shape=bf16(2, 4096, 256),
        in_specs=[SMEM] + [VMEM] * 9,
        out_specs=VMEM,
        compiler_params=room(10),
        name="rows",
        cost_estimate=pl.CostEstimate(flops=30_000_000_000, bytes_accessed=8_000_000, transcendentals=0),
    )(pos, z_tile, *z_plus, *z_minus, *z_far)
    p_own, p_peer = pl.pallas_call(
        near_kernel,
        out_shape=[f32(1024, 256), f32(1024, 256)],
        in_specs=[VMEM] * 4,
        out_specs=[VMEM, VMEM],
        compiler_params=room(14),
        name="near",
        cost_estimate=pl.CostEstimate(flops=3_200_000_000, bytes_accessed=12_000_000, transcendentals=0),
    )(inner, line, line_p, line_m)
    keep = keep_mask.T
    peer_part, parts = pl.pallas_call(
        far_peer_kernel,
        out_shape=[f32(1024, 256), f32(1, BLK)],
        in_specs=[SMEM, SMEM, SMEM] + [VMEM] * 6,
        out_specs=[VMEM, VMEM],
        compiler_params=room(14),
        name="far_peer",
        cost_estimate=pl.CostEstimate(flops=540_000_000, bytes_accessed=4_000_000, transcendentals=0),
    )(pos, keep, branch_flag, m, inner, q0, q1, p_own, p_peer)
    own_part = pl.pallas_call(
        far_own_kernel,
        out_shape=f32(1024, 256),
        in_specs=[VMEM] * 5,
        out_specs=VMEM,
        compiler_params=room(10),
        name="far_own",
        cost_estimate=pl.CostEstimate(flops=540_000_000, bytes_accessed=4_000_000, transcendentals=0),
    )(inner, q0, q1, p_own, parts)
    recv = lax.ppermute(peer_part, "layer", swap)
    updated = pl.pallas_call(
        final_kernel,
        out_shape=f32(1024, 256),
        in_specs=[SMEM, SMEM, VMEM, VMEM, VMEM],
        out_specs=VMEM,
        compiler_params=room(6),
        name="final",
        cost_estimate=pl.CostEstimate(flops=2_000_000, bytes_accessed=4_000_000, transcendentals=0),
    )(keep, branch_flag, own_part, recv, m)
    return (updated, trace_of(parts))


def solution(mesh):
    split = Mesh(
        mesh.devices.reshape(mesh.shape["row"], 4, 4, mesh.shape["layer"]),
        ("row", Y, X, "layer"),
    )
    in_specs = (P("row", COL_LAYER), P("row", COL_LAYER), P("row", COL_LAYER), P("row"))
    out_specs = (P("row", COL_LAYER), P())
    return jax.shard_map(
        on_device, mesh=split, in_specs=in_specs, out_specs=out_specs, check_vma=False
    )
```

time: 123 us -> 104 us (0.85)
  starting transfers between devices: 44.3 us -> 33.3 us
  Pallas kernels: 16.7 us -> 9.67 us
  waiting for transfers between devices: 33.5 us -> 36.8 us
  local copies, waits for them, and re-layouts: 4.19 us -> 2.16 us
  blocking collectives: 22.3 us -> 20.3 us
    ppermute x24 -> x8, starting transfers between devices: 32.7 us -> 15.7 us  [shift(): return lax.ppermute(value, axis, [(i, (i + off) % n) for i in range(n)])]
    pallas_call x4 -> x12, Pallas kernels: 16.7 us -> 9.67 us  [the longest x1 3.9 us: on_device(): pl.pallas_call(near_kernel, out_shape=[f32(1024, 256), f32(1024, 256)], i...]
    ppermute x2 -> x10, starting transfers between devices: 8.29 us -> 14.3 us  [the longest x8 9.01 us: turn(): return lax.ppermute(value, ('row', Y, X, 'layer'), pairs)]
    ppermute x2 -> x10, waiting for transfers between devices: 3.24 us -> 8.84 us  [the longest x8 8.72 us: turn(): return lax.ppermute(value, ('row', Y, X, 'layer'), pairs)]
    all_to_all x2 -> x1, blocking collectives: 22.3 us -> 20.3 us  [trace_of(): lax.all_to_all(spread, ('row', Y, X), 0, 0).reshape(8, 16, BLK).sum(axis=1)]
    unnamed x32 -> x13, local copies, waits for them, and re-layouts: 3.92 us -> 1.88 us
    ppermute x24 -> x8, waiting for transfers between devices: 29.1 us -> 28 us  [shift(): return lax.ppermute(value, axis, [(i, (i + off) % n) for i in range(n)])]
  transfers between devices with their start and end apart: 27 -> 19, of which waited for: 9 -> 9; matrix products, arithmetic and copies ran while one was open for 0% -> 1% of each run, Pallas kernels for 8% -> 5%
where the time goes in v2:
time: 104 us
  waiting for transfers between devices  36.8 us (35%)
  starting transfers between devices  33.3 us (32%)
  blocking collectives  20.3 us (20%)
  Pallas kernels  9.67 us (9%)
  local copies, waits for them, and re-layouts  2.16 us (2%)
    ppermute x8, waiting for transfers between devices, shift(): return lax.ppermute(value, axis, [(i, (i + off) % n) for i in range(n)])  28 us
    all_to_all x1, blocking collectives, trace_of(): lax.all_to_all(spread, ('row', Y, X), 0, 0).reshape(8, 16, BLK).sum(axis=1)  20.3 us
    ppermute x8, starting transfers between devices, shift(): return lax.ppermute(value, axis, [(i, (i + off) % n) for i in range(n)])  15.7 us
    ppermute x8, starting transfers between devices, turn(): return lax.ppermute(value, ('row', Y, X, 'layer'), pairs)  9.01 us
    ppermute x8, waiting for transfers between devices, turn(): return lax.ppermute(value, ('row', Y, X, 'layer'), pairs)  8.72 us
    pallas_call x1, Pallas kernels, on_device(): pl.pallas_call(near_kernel, out_shape=[f32(1024, 256), f32(1024, 256)], i...  3.9 us
    ppermute x1, starting transfers between devices, on_device(): recv = lax.ppermute(peer_part, 'layer', swap)  3.78 us
    ppermute x1, starting transfers between devices, on_device(): other = lax.ppermute(peer_rows, 'layer', swap)  3.32 us
  transfers between devices with their start and end apart: 19, of which 9 were waited for; matrix products, arithmetic and copies ran while one was open for 1% of the time, Pallas kernels for 5%

profile of v2, /device:TPU:1, one launch (start us, length us, event | category | flops | bytes accessed | tf_op | source)
XLA Modules:
  0.0 103.8 jit_solution(317312977182822695)
XLA Ops:
  0.6 0.1 pad_add_fusion.pos
  0.7 1.0 %copy-done = bf16[1024,256]{1,0:T(8,128)(2,1)S(1)} copy-done((bf16[1024,256]{1,0:T(8,128)(2,1)S(1)}, bf16[1024,256]{1,0:T(8,128)(2,1)}, u32[]{:S(2)}) %copy-start) | copy-done | bytes 524312
  1.8 0.7 copy-done.3
  2.4 0.7 mask.1
  3.2 3.3 %collective-permute-start = (bf16[2,256,256]{2,1,0:T(8,128)(2,1)S(1)}, bf16[2,256,256]{2,1,0:T(8,128)(2,1)S(1)}, u32[]{:S(2)}, u32[]{:S(2)}) collective-permute-start(bf16[2,256,256]{2,1,0:T(8,128)(2,1)S(1)} %get-tuple-element.10), channel_id=1, source_target_pairs={{0,1},{1,0},{2,3},{3,2},{4,5},{5,4},{6,7},{7,6},{8,9},{9,8},{10,11... | collective-permute-start | bytes 786440 | tf_op jit(solution)/shard_map/ppermute | solution.py:213
  6.5 1.0 collective-permute-start.10
  7.5 0.5 collective-permute-start.9
  8.0 5.2 %collective-permute-start.4 = (bf16[4,256,256]{2,1,0:T(8,128)(2,1)S(1)}, bf16[4,256,256]{2,1,0:T(8,128)(2,1)S(1)}, u32[]{:S(2)}, u32[]{:S(2)}) collective-permute-start(bf16[4,256,256]{2,1,0:T(8,128)(2,1)S(1)} %constant_dynamic-update-slice_fusion.refs_0_), channel_id=1, source_target_pairs={{0,224},{32,0},{64,32},{96,64},{128,96},{160,128},{192,160},{224,1... | collective-permute-start | bytes 1572872 | tf_op jit(solution)/shard_map/ppermute | solution.py:25
  13.3 0.1 collective-permute-start.1
  13.4 1.4 %collective-permute-done.10 = bf16[1024,256]{1,0:T(8,128)(2,1)S(1)} collective-permute-done((bf16[1024,256]{1,0:T(8,128)(2,1)S(1)}, bf16[1024,256]{1,0:T(8,128)(2,1)S(1)}, u32[]{:S(2)}, u32[]{:S(2)}) %collective-permute-start.10) | collective-permute-done | bytes 524320 | tf_op jit(solution)/shard_map/ppermute | solution.py:39
  14.9 2.3 %collective-permute-start.12 = (bf16[512,256]{1,0:T(8,128)(2,1)S(1)}, bf16[512,256]{1,0:T(8,128)(2,1)S(1)}, u32[]{:S(2)}, u32[]{:S(2)}) collective-permute-start(bf16[512,256]{1,0:T(8,128)(2,1)S(1)} %slice.43), channel_id=1, source_target_pairs={{0,6},{1,25},{2,0},{3,27},{4,2},{5,29},{6,4},{7,31},{8,14},{9,1},{... | collective-permute-start | bytes 786440 | tf_op jit(solution)/shard_map/ppermute | solution.py:39
  17.1 0.0 collective-permute-done.9
  17.2 0.1 collective-permute-start.11
  17.4 7.2 %collective-permute-done.4.x = bf16[4,256,256]{2,1,0:T(8,128)(2,1)S(1)} collective-permute-done((bf16[4,256,256]{2,1,0:T(8,128)(2,1)S(1)}, bf16[4,256,256]{2,1,0:T(8,128)(2,1)S(1)}, u32[]{:S(2)}, u32[]{:S(2)}) %collective-permute-start.4) | collective-permute-done | bytes 524320 | tf_op jit(solution)/shard_map/ppermute | solution.py:25
  24.5 3.4 %collective-permute-start.5 = (bf16[4,256,256]{2,1,0:T(8,128)(2,1)S(1)}, bf16[4,256,256]{2,1,0:T(8,128)(2,1)S(1)}, u32[]{:S(2)}, u32[]{:S(2)}) collective-permute-start(bf16[4,256,256]{2,1,0:T(8,128)(2,1)S(1)} %hold.9.refs_4_), channel_id=1, source_target_pairs={{0,224},{32,0},{64,32},{96,64},{128,96},{160,128},{192,160},{224,1... | collective-permute-start | bytes 1572872 | tf_op jit(solution)/shard_map/ppermute | solution.py:25
  28.0 1.9 %collective-permute-start.15 = (bf16[4096,256]{1,0:T(8,128)(2,1)S(1)}, bf16[4096,256]{1,0:T(8,128)(2,1)S(1)}, u32[]{:S(2)}, u32[]{:S(2)}) collective-permute-start(bf16[4096,256]{1,0:T(8,128)(2,1)S(1)} %constant_dynamic-update-slice_fusion.2.line), channel_id=1, source_target_pairs={{0,24},{1,7},{2,26},{3,1},{4,28},{5,3},{6,30},{7,5},{8,0},{9,15},{... | collective-permute-start | bytes 6291464 | tf_op jit(solution)/shard_map/ppermute | solution.py:39
  29.9 0.0 collective-permute-done.1.x
  30.0 0.0 collective-permute-start.2
  30.0 8.3 %collective-permute-done.5.x = bf16[4,256,256]{2,1,0:T(8,128)(2,1)S(1)} collective-permute-done((bf16[4,256,256]{2,1,0:T(8,128)(2,1)S(1)}, bf16[4,256,256]{2,1,0:T(8,128)(2,1)S(1)}, u32[]{:S(2)}, u32[]{:S(2)}) %collective-permute-start.5) | collective-permute-done | bytes 524320 | tf_op jit(solution)/shard_map/ppermute | solution.py:25
  38.3 3.4 %collective-permute-start.6 = (bf16[4,256,256]{2,1,0:T(8,128)(2,1)S(1)}, bf16[4,256,256]{2,1,0:T(8,128)(2,1)S(1)}, u32[]{:S(2)}, u32[]{:S(2)}) collective-permute-start(bf16[4,256,256]{2,1,0:T(8,128)(2,1)S(1)} %hold.10.refs_5_), channel_id=1, source_target_pairs={{0,224},{32,0},{64,32},{96,64},{128,96},{160,128},{192,160},{224,1... | collective-permute-start | bytes 1572872 | tf_op jit(solution)/shard_map/ppermute | solution.py:25
  41.7 0.7 collective-permute-done.2.x
  42.4 8.8 %collective-permute-done.6.x = bf16[4,256,256]{2,1,0:T(8,128)(2,1)S(1)} collective-permute-done((bf16[4,256,256]{2,1,0:T(8,128)(2,1)S(1)}, bf16[4,256,256]{2,1,0:T(8,128)(2,1)S(1)}, u32[]{:S(2)}, u32[]{:S(2)}) %collective-permute-start.6) | collective-permute-done | bytes 524320 | tf_op jit(solution)/shard_map/ppermute | solution.py:25
  51.2 3.5 %collective-permute-start.8 = (bf16[2,256,256]{2,1,0:T(8,128)(2,1)S(1)}, bf16[2,256,256]{2,1,0:T(8,128)(2,1)S(1)}, u32[]{:S(2)}, u32[]{:S(2)}) collective-permute-start(bf16[2,256,256]{2,1,0:T(8,128)(2,1)S(1)} %slice.41), channel_id=1, source_target_pairs={{0,224},{32,0},{64,32},{96,64},{128,96},{160,128},{192,160},{224,1... | collective-permute-start | bytes 786440 | tf_op jit(solution)/shard_map/ppermute | solution.py:25
  54.7 0.0 collective-permute-done.3.x
  54.7 0.1 collective-permute-start.7
  54.8 0.0 collective-permute-done.15.line_m
  54.8 0.1 slice.45
  54.9 3.2 %collective-permute-start.16 = (bf16[2048,256]{1,0:T(8,128)(2,1)S(1)}, bf16[2048,256]{1,0:T(8,128)(2,1)S(1)}, u32[]{:S(2)}, u32[]{:S(2)}) collective-permute-start(bf16[2048,256]{1,0:T(8,128)(2,1)S(1)} %slice.45), channel_id=1, source_target_pairs={{0,24},{1,7},{2,26},{3,1},{4,28},{5,3},{6,30},{7,5},{8,0},{9,15},{... | collective-permute-start | bytes 3145736 | tf_op jit(solution)/shard_map/ppermute | solution.py:39
  58.0 0.0 collective-permute-done.13.line_p
  58.0 0.1 slice.44
  58.1 0.1 collective-permute-start.14
  58.2 0.0 collective-permute-done.8.refs_8_
  58.2 3.0 %collective-permute-done.7.refs_7_ = bf16[2,256,256]{2,1,0:T(8,128)(2,1)S(1)} collective-permute-done((bf16[2,256,256]{2,1,0:T(8,128)(2,1)S(1)}, bf16[2,256,256]{2,1,0:T(8,128)(2,1)S(1)}, u32[]{:S(2)}, u32[]{:S(2)}) %collective-permute-start.7) | collective-permute-done | bytes 262176 | tf_op jit(solution)/shard_map/ppermute | solution.py:25
  61.2 0.9 rows.1.b
  62.1 0.0 copy-start.1
  62.2 0.0 copy-start.2
  62.2 3.9 %near.1 = (f32[1024,256]{1,0:T(8,128)S(1)}, f32[1024,256]{1,0:T(8,128)S(1)}) custom-call(bf16[2,4096,256]{2,1,0:T(8,128)(2,1)S(1)} %rows.1.b, bf16[4096,256]{1,0:T(8,128)(2,1)S(1)} %constant_dynamic-update-slice_fusion.2.line, bf16[4096,256]{1,0:T(8,128)(2,1)S(1)} %collective-permute-done.13.line_p, bf16[4096,256]{1,0:T(8,128)(2,1)S(1)} %collective-permute-done.15.line_m), custom_call_target="tpu_custom_call" | custom-call | flops 3200000000 | bytes 12000000 | tf_op jit(solution)/shard_map/near/pallas_call | solution.py:227
  66.1 4.0 %collective-permute-done.16.q1 = bf16[2048,256]{1,0:T(8,128)(2,1)S(1)} collective-permute-done((bf16[2048,256]{1,0:T(8,128)(2,1)S(1)}, bf16[2048,256]{1,0:T(8,128)(2,1)S(1)}, u32[]{:S(2)}, u32[]{:S(2)}) %collective-permute-start.16) | collective-permute-done | bytes 1048608 | tf_op jit(solution)/shard_map/ppermute | solution.py:39
  70.0 3.3 %collective-permute-done.14.q0 = bf16[2048,256]{1,0:T(8,128)(2,1)S(1)} collective-permute-done((bf16[2048,256]{1,0:T(8,128)(2,1)S(1)}, bf16[2048,256]{1,0:T(8,128)(2,1)S(1)}, u32[]{:S(2)}, u32[]{:S(2)}) %collective-permute-start.14) | collective-permute-done | bytes 1048608 | tf_op jit(solution)/shard_map/ppermute | solution.py:39
  73.3 1.6 %far_peer.1 = (f32[1024,256]{1,0:T(8,128)S(1)}, f32[1,128]{1,0:T(1,128)S(1)}) custom-call(s32[4]{0:T(128)S(1)} %pad_add_fusion.pos, s32[2,8]{1,0:T(2,128)S(1)} %bitcast.10, s32[8]{0:T(128)S(1)} %copy-done.2, bf16[1024,256]{1,0:T(8,128)(2,1)S(1)} %get-tuple-element.11.m, bf16[2,4096,256]{2,1,0:T(8,128)(2,1)S(1)} %rows.1.b, ...), custom_call_target="tpu_custom_call" | custom-call | flops 540000000 | bytes 4000000 | tf_op jit(solution)/shard_map/far_peer/pallas_call | solution.py:237
  75.0 3.8 %collective-permute-start.17 = (f32[1024,256]{1,0:T(8,128)S(1)}, f32[1024,256]{1,0:T(8,128)S(1)}, u32[]{:S(2)}, u32[]{:S(2)}) collective-permute-start(f32[1024,256]{1,0:T(8,128)S(1)} %get-tuple-element.15), channel_id=1, source_target_pairs={{0,1},{1,0},{2,3},{3,2},{4,5},{5,4},{6,7},{7,6},{8,9},{9,8},{10,11... | collective-permute-start | bytes 3145736 | tf_op jit(solution)/shard_map/ppermute | solution.py:255
  78.8 20.3 %all_to_all.5 = f32[128,1,128]{2,1,0:T(1,128)S(1)} all-to-all(f32[128,1,128]{2,1,0:T(1,128)S(1)} %broadcast_in_dim.9), channel_id=1, replica_groups=mesh['row'=8,'col_0'=4,'col_1'=4,'layer'=2] {'row','col_0','col_1'}, dimensions={0} | all-to-all | bytes 131072 | tf_op jit(solution)/shard_map/all_to_all | solution.py:196
  99.1 1.5 %collective-permute-start.18 = (f32[8,128]{1,0:T(8,128)S(1)}, f32[8,128]{1,0:T(8,128)S(1)}, u32[]{:S(2)}, u32[]{:S(2)}) collective-permute-start(f32[8,128]{1,0:T(8,128)S(1)} %bitcast_reduce_fusion), channel_id=1, source_target_pairs={{0,1},{1,0},{2,3},{3,2},{4,5},{5,4},{6,7},{7,6},{8,9},{9,8},{10,11... | collective-permute-start | bytes 12296 | tf_op jit(solution)/shard_map/ppermute | solution.py:197
  100.6 0.7 far_own.1.own
  101.3 0.1 collective-permute-done.18
  101.4 0.7 fusion.1
  102.1 0.0 collective-permute-done.17.recv
  102.1 1.8 %final.1 = f32[1024,256]{1,0:T(8,128)} custom-call(s32[2,8]{1,0:T(2,128)S(1)} %bitcast.11, s32[8]{0:T(128)S(1)} %copy-done.2, f32[1024,256]{1,0:T(8,128)S(1)} %far_own.1.own, f32[1024,256]{1,0:T(8,128)S(1)} %collective-permute-done.17.recv, bf16[1024,256]{1,0:T(8,128)(2,1)S(1)} %get-tuple-element.11.m), custom_call_target="tpu_custom_call" | custom-call | flops 2000000 | bytes 4000000 | tf_op jit(solution)/shard_map/final/pallas_call | solution.py:256
  (29 shorter events, 0.3 us)
Async XLA Ops:
  0.7 1.0 %copy-start = (bf16[1024,256]{1,0:T(8,128)(2,1)S(1)}, bf16[1024,256]{1,0:T(8,128)(2,1)}, u32[]{:S(2)}) copy-start(bf16[1024,256]{1,0:T(8,128)(2,1)} %x.1) | copy-start | bytes 1572868
  1.8 0.7 copy-start.3
  3.2 4.8 %collective-permute-start = (bf16[2,256,256]{2,1,0:T(8,128)(2,1)S(1)}, bf16[2,256,256]{2,1,0:T(8,128)(2,1)S(1)}, u32[]{:S(2)}, u32[]{:S(2)}) collective-permute-start(bf16[2,256,256]{2,1,0:T(8,128)(2,1)S(1)} %get-tuple-element.10), channel_id=1, source_target_pairs={{0,1},{1,0},{2,3},{3,2},{4,5},{5,4},{6,7},{7,6},{8,9},{9,8},{10,11... | collective-permute-start | bytes 786440 | tf_op jit(solution)/shard_map/ppermute | solution.py:213
  6.5 8.3 %collective-permute-start.10 = (bf16[1024,256]{1,0:T(8,128)(2,1)S(1)}, bf16[1024,256]{1,0:T(8,128)(2,1)S(1)}, u32[]{:S(2)}, u32[]{:S(2)}) collective-permute-start(bf16[1024,256]{1,0:T(8,128)(2,1)S(1)} %get-tuple-element.11.m), channel_id=1, source_target_pairs={{0,6},{1,25},{2,0},{3,27},{4,2},{5,29},{6,4},{7,31},{8,14},{9,1},{... | collective-permute-start | bytes 1572872 | tf_op jit(solution)/shard_map/ppermute | solution.py:39
  7.5 9.6 %collective-permute-start.9 = (bf16[1024,256]{1,0:T(8,128)(2,1)S(1)}, bf16[1024,256]{1,0:T(8,128)(2,1)S(1)}, u32[]{:S(2)}, u32[]{:S(2)}) collective-permute-start(bf16[1024,256]{1,0:T(8,128)(2,1)S(1)} %get-tuple-element.11.m), channel_id=1, source_target_pairs={{0,2},{1,9},{2,4},{3,11},{4,6},{5,13},{6,0},{7,15},{8,10},{9,17},{... | collective-permute-start | bytes 1572872 | tf_op jit(solution)/shard_map/ppermute | solution.py:39
  8.0 16.5 %collective-permute-start.4 = (bf16[4,256,256]{2,1,0:T(8,128)(2,1)S(1)}, bf16[4,256,256]{2,1,0:T(8,128)(2,1)S(1)}, u32[]{:S(2)}, u32[]{:S(2)}) collective-permute-start(bf16[4,256,256]{2,1,0:T(8,128)(2,1)S(1)} %constant_dynamic-update-slice_fusion.refs_0_), channel_id=1, source_target_pairs={{0,224},{32,0},{64,32},{96,64},{128,96},{160,128},{192,160},{224,1... | collective-permute-start | bytes 1572872 | tf_op jit(solution)/shard_map/ppermute | solution.py:25
  13.3 16.7 %collective-permute-start.1 = (bf16[4,256,256]{2,1,0:T(8,128)(2,1)S(1)}, bf16[4,256,256]{2,1,0:T(8,128)(2,1)S(1)}, u32[]{:S(2)}, u32[]{:S(2)}) collective-permute-start(bf16[4,256,256]{2,1,0:T(8,128)(2,1)S(1)} %constant_dynamic-update-slice_fusion.refs_0_), channel_id=1, source_target_pairs={{0,32},{32,64},{64,96},{96,128},{128,160},{160,192},{192,224},{224... | collective-permute-start | bytes 1572872 | tf_op jit(solution)/shard_map/ppermute | solution.py:25
  14.9 13.1 %collective-permute-start.12 = (bf16[512,256]{1,0:T(8,128)(2,1)S(1)}, bf16[512,256]{1,0:T(8,128)(2,1)S(1)}, u32[]{:S(2)}, u32[]{:S(2)}) collective-permute-start(bf16[512,256]{1,0:T(8,128)(2,1)S(1)} %slice.43), channel_id=1, source_target_pairs={{0,6},{1,25},{2,0},{3,27},{4,2},{5,29},{6,4},{7,31},{8,14},{9,1},{... | collective-permute-start | bytes 786440 | tf_op jit(solution)/shard_map/ppermute | solution.py:39
  17.2 10.8 %collective-permute-start.11 = (bf16[512,256]{1,0:T(8,128)(2,1)S(1)}, bf16[512,256]{1,0:T(8,128)(2,1)S(1)}, u32[]{:S(2)}, u32[]{:S(2)}) collective-permute-start(bf16[512,256]{1,0:T(8,128)(2,1)S(1)} %slice.42), channel_id=1, source_target_pairs={{0,2},{1,9},{2,4},{3,11},{4,6},{5,13},{6,0},{7,15},{8,10},{9,17},{... | collective-permute-start | bytes 786440 | tf_op jit(solution)/shard_map/ppermute | solution.py:39
  24.5 13.8 %collective-permute-start.5 = (bf16[4,256,256]{2,1,0:T(8,128)(2,1)S(1)}, bf16[4,256,256]{2,1,0:T(8,128)(2,1)S(1)}, u32[]{:S(2)}, u32[]{:S(2)}) collective-permute-start(bf16[4,256,256]{2,1,0:T(8,128)(2,1)S(1)} %hold.9.refs_4_), channel_id=1, source_target_pairs={{0,224},{32,0},{64,32},{96,64},{128,96},{160,128},{192,160},{224,1... | collective-permute-start | bytes 1572872 | tf_op jit(solution)/shard_map/ppermute | solution.py:25
  28.0 26.8 %collective-permute-start.15 = (bf16[4096,256]{1,0:T(8,128)(2,1)S(1)}, bf16[4096,256]{1,0:T(8,128)(2,1)S(1)}, u32[]{:S(2)}, u32[]{:S(2)}) collective-permute-start(bf16[4096,256]{1,0:T(8,128)(2,1)S(1)} %constant_dynamic-update-slice_fusion.2.line), channel_id=1, source_target_pairs={{0,24},{1,7},{2,26},{3,1},{4,28},{5,3},{6,30},{7,5},{8,0},{9,15},{... | collective-permute-start | bytes 6291464 | tf_op jit(solution)/shard_map/ppermute | solution.py:39
  29.9 28.1 %collective-permute-start.13 = (bf16[4096,256]{1,0:T(8,128)(2,1)S(1)}, bf16[4096,256]{1,0:T(8,128)(2,1)S(1)}, u32[]{:S(2)}, u32[]{:S(2)}) collective-permute-start(bf16[4096,256]{1,0:T(8,128)(2,1)S(1)} %constant_dynamic-update-slice_fusion.2.line), channel_id=1, source_target_pairs={{0,8},{1,3},{2,10},{3,5},{4,12},{5,7},{6,14},{7,1},{8,16},{9,11},{... | collective-permute-start | bytes 6291464 | tf_op jit(solution)/shard_map/ppermute | solution.py:39
  30.0 12.4 %collective-permute-start.2 = (bf16[4,256,256]{2,1,0:T(8,128)(2,1)S(1)}, bf16[4,256,256]{2,1,0:T(8,128)(2,1)S(1)}, u32[]{:S(2)}, u32[]{:S(2)}) collective-permute-start(bf16[4,256,256]{2,1,0:T(8,128)(2,1)S(1)} %hold.6.refs_1_), channel_id=1, source_target_pairs={{0,32},{32,64},{64,96},{96,128},{128,160},{160,192},{192,224},{224... | collective-permute-start | bytes 1572872 | tf_op jit(solution)/shard_map/ppermute | solution.py:25
  38.3 12.9 %collective-permute-start.6 = (bf16[4,256,256]{2,1,0:T(8,128)(2,1)S(1)}, bf16[4,256,256]{2,1,0:T(8,128)(2,1)S(1)}, u32[]{:S(2)}, u32[]{:S(2)}) collective-permute-start(bf16[4,256,256]{2,1,0:T(8,128)(2,1)S(1)} %hold.10.refs_5_), channel_id=1, source_target_pairs={{0,224},{32,0},{64,32},{96,64},{128,96},{160,128},{192,160},{224,1... | collective-permute-start | bytes 1572872 | tf_op jit(solution)/shard_map/ppermute | solution.py:25
  42.4 12.3 %collective-permute-start.3 = (bf16[4,256,256]{2,1,0:T(8,128)(2,1)S(1)}, bf16[4,256,256]{2,1,0:T(8,128)(2,1)S(1)}, u32[]{:S(2)}, u32[]{:S(2)}) collective-permute-start(bf16[4,256,256]{2,1,0:T(8,128)(2,1)S(1)} %hold.7.refs_2_), channel_id=1, source_target_pairs={{0,32},{32,64},{64,96},{96,128},{128,160},{160,192},{192,224},{224... | collective-permute-start | bytes 1572872 | tf_op jit(solution)/shard_map/ppermute | solution.py:25
  51.2 7.0 %collective-permute-start.8 = (bf16[2,256,256]{2,1,0:T(8,128)(2,1)S(1)}, bf16[2,256,256]{2,1,0:T(8,128)(2,1)S(1)}, u32[]{:S(2)}, u32[]{:S(2)}) collective-permute-start(bf16[2,256,256]{2,1,0:T(8,128)(2,1)S(1)} %slice.41), channel_id=1, source_target_pairs={{0,224},{32,0},{64,32},{96,64},{128,96},{160,128},{192,160},{224,1... | collective-permute-start | bytes 786440 | tf_op jit(solution)/shard_map/ppermute | solution.py:25
  54.7 6.5 %collective-permute-start.7 = (bf16[2,256,256]{2,1,0:T(8,128)(2,1)S(1)}, bf16[2,256,256]{2,1,0:T(8,128)(2,1)S(1)}, u32[]{:S(2)}, u32[]{:S(2)}) collective-permute-start(bf16[2,256,256]{2,1,0:T(8,128)(2,1)S(1)} %slice.40), channel_id=1, source_target_pairs={{0,32},{32,64},{64,96},{96,128},{128,160},{160,192},{192,224},{224... | collective-permute-start | bytes 786440 | tf_op jit(solution)/shard_map/ppermute | solution.py:25
  54.9 15.2 %collective-permute-start.16 = (bf16[2048,256]{1,0:T(8,128)(2,1)S(1)}, bf16[2048,256]{1,0:T(8,128)(2,1)S(1)}, u32[]{:S(2)}, u32[]{:S(2)}) collective-permute-start(bf16[2048,256]{1,0:T(8,128)(2,1)S(1)} %slice.45), channel_id=1, source_target_pairs={{0,24},{1,7},{2,26},{3,1},{4,28},{5,3},{6,30},{7,5},{8,0},{9,15},{... | collective-permute-start | bytes 3145736 | tf_op jit(solution)/shard_map/ppermute | solution.py:39
  58.1 15.2 %collective-permute-start.14 = (bf16[2048,256]{1,0:T(8,128)(2,1)S(1)}, bf16[2048,256]{1,0:T(8,128)(2,1)S(1)}, u32[]{:S(2)}, u32[]{:S(2)}) collective-permute-start(bf16[2048,256]{1,0:T(8,128)(2,1)S(1)} %slice.44), channel_id=1, source_target_pairs={{0,8},{1,3},{2,10},{3,5},{4,12},{5,7},{6,14},{7,1},{8,16},{9,11},{... | collective-permute-start | bytes 3145736 | tf_op jit(solution)/shard_map/ppermute | solution.py:39
  62.1 11.2 %copy-start.1 = (s32[8,2]{0,1:T(2,128)S(1)}, s32[8,2]{0,1:T(2,128)}, u32[]{:S(2)}) copy-start(s32[8,2]{0,1:T(2,128)} %param.6) | copy-start | bytes 196
  62.2 11.2 %copy-start.2 = (s32[8]{0:T(128)S(1)}, s32[8]{0:T(128)}, u32[]{:S(2)}) copy-start(s32[8]{0:T(128)} %flag.3) | copy-start | bytes 100
  75.0 27.1 %collective-permute-start.17 = (f32[1024,256]{1,0:T(8,128)S(1)}, f32[1024,256]{1,0:T(8,128)S(1)}, u32[]{:S(2)}, u32[]{:S(2)}) collective-permute-start(f32[1024,256]{1,0:T(8,128)S(1)} %get-tuple-element.15), channel_id=1, source_target_pairs={{0,1},{1,0},{2,3},{3,2},{4,5},{5,4},{6,7},{7,6},{8,9},{9,8},{10,11... | collective-permute-start | bytes 3145736 | tf_op jit(solution)/shard_map/ppermute | solution.py:255
  99.1 2.3 %collective-permute-start.18 = (f32[8,128]{1,0:T(8,128)S(1)}, f32[8,128]{1,0:T(8,128)S(1)}, u32[]{:S(2)}, u32[]{:S(2)}) collective-permute-start(f32[8,128]{1,0:T(8,128)S(1)} %bitcast_reduce_fusion), channel_id=1, source_target_pairs={{0,1},{1,0},{2,3},{3,2},{4,5},{5,4},{6,7},{7,6},{8,9},{9,8},{10,11... | collective-permute-start | bytes 12296 | tf_op jit(solution)/shard_map/ppermute | solution.py:197

commit v3 on v2

--- a/solution.py
+++ b/solution.py
@@ -9,6 +9,8 @@
 from jax.sharding import PartitionSpec as P
 
 BLK = 128
+HZ = (6.0, 6.0, 2.0)
+HR = 2.0
 Y, X = "col_0", "col_1"
 COL_LAYER = (Y, X, "layer")
 SMEM = pl.BlockSpec(memory_space=pltpu.SMEM)
@@ -63,13 +65,16 @@
 
 
 def ring8(own, axis):
-    half = own.shape[0] // 2
     plus, minus = [own], [own]
-    for _ in range(3):
-        plus.append(hold(shift(plus[-1], axis, 1), 4.0))
-        minus.append(hold(shift(minus[-1], axis, -1), 4.0))
-    far = (shift(plus[-1][:half], axis, 1), shift(minus[-1][half:], axis, -1))
-    return plus[1:], minus[1:], far
+    for cost in HZ:
+        plus.append(hold(shift(plus[-1], axis, 1), cost))
+        minus.append(hold(shift(minus[-1], axis, -1), cost))
+    return plus[1:], minus[1:]
+
+
+def ring8_end(plus, minus, axis):
+    half = plus.shape[0] // 2
+    return shift(plus[:half], axis, 1), shift(minus[half:], axis, -1)
 
 
 def mask_kernel(pos, bm, x, m, own, peer):
@@ -212,9 +217,12 @@
     )(pos, block_mask.T, density)
     other = lax.ppermute(peer_rows, "layer", swap)
     z_tile = jnp.concatenate([own_rows, other], axis=0)
-    z_plus, z_minus, z_far = ring8(z_tile, "row")
-    line = jnp.concatenate([m, *ring4(m, 0)], axis=0)
+    z_plus, z_minus = ring8(z_tile, "row")
+    line = jnp.concatenate([m, *(turn(m, 0, off) for off in (1, -1, 2))], axis=0)
     line_p, line_m, q0, q1 = ring4(line, 1)
+    z_plus[2], _ = lax.optimization_barrier((z_plus[2], line_p))
+    z_minus[2], _ = lax.optimization_barrier((z_minus[2], line_m))
+    z_far = ring8_end(z_plus[2], z_minus[2], "row")
     inner = pl.pallas_call(
         rows_kernel,
         out_shape=bf16(2, 4096, 256),
@@ -222,7 +230,7 @@
         out_specs=VMEM,
         compiler_params=room(10),
         name="rows",
-        cost_estimate=pl.CostEstimate(flops=30_000_000_000, bytes_accessed=8_000_000, transcendentals=0),
+        cost_estimate=pl.CostEstimate(flops=int(HR * 1e9), bytes_accessed=8_000_000, transcendentals=0),
     )(pos, z_tile, *z_plus, *z_minus, *z_far)
     p_own, p_peer = pl.pallas_call(
         near_kernel,

time: 104 us -> 100 us (0.962)
  waiting for transfers between devices: 36.8 us -> 33.8 us
  blocking collectives: 20.3 us -> 19.1 us
    ppermute x8, waiting for transfers between devices: 28 us -> 19.2 us  [shift(): return lax.ppermute(value, axis, [(i, (i + off) % n) for i in range(n)])]
    ppermute x8 -> x7, waiting for transfers between devices: 8.72 us -> 14.6 us  [turn(): return lax.ppermute(value, ('row', Y, X, 'layer'), pairs)]
    ppermute x8, starting transfers between devices: 15.7 us -> 17.5 us  [shift(): return lax.ppermute(value, axis, [(i, (i + off) % n) for i in range(n)])]
    ppermute x8 -> x7, starting transfers between devices: 9.01 us -> 7.33 us  [turn(): return lax.ppermute(value, ('row', Y, X, 'layer'), pairs)]
    all_to_all x1, blocking collectives: 20.3 us -> 19.1 us  [trace_of(): lax.all_to_all(spread, ('row', Y, X), 0, 0).reshape(8, 16, BLK).sum(axis=1)]
  transfers between devices with their start and end apart: 19 -> 18, of which waited for: 9 -> 8; matrix products, arithmetic and copies ran while one was open for 1% -> 1% of each run, Pallas kernels for 5% -> 6%
where the time goes in v3:
time: 100 us
  starting transfers between devices  33.8 us (34%)
  waiting for transfers between devices  33.8 us (34%)
  blocking collectives  19.1 us (19%)
  Pallas kernels  9.67 us (10%)
  local copies, waits for them, and re-layouts  2.12 us (2%)
    ppermute x8, waiting for transfers between devices, shift(): return lax.ppermute(value, axis, [(i, (i + off) % n) for i in range(n)])  19.2 us
    all_to_all x1, blocking collectives, trace_of(): lax.all_to_all(spread, ('row', Y, X), 0, 0).reshape(8, 16, BLK).sum(axis=1)  19.1 us
    ppermute x8, starting transfers between devices, shift(): return lax.ppermute(value, axis, [(i, (i + off) % n) for i in range(n)])  17.5 us
    ppermute x7, waiting for transfers between devices, turn(): return lax.ppermute(value, ('row', Y, X, 'layer'), pairs)  14.6 us
    ppermute x7, starting transfers between devices, turn(): return lax.ppermute(value, ('row', Y, X, 'layer'), pairs)  7.33 us
    ppermute x1, starting transfers between devices, on_device(): recv = lax.ppermute(peer_part, 'layer', swap)  4.1 us
    pallas_call x1, Pallas kernels, on_device(): pl.pallas_call(near_kernel, out_shape=[f32(1024, 256), f32(1024, 256)], i...  3.9 us
    ppermute x1, starting transfers between devices, on_device(): other = lax.ppermute(peer_rows, 'layer', swap)  3.32 us
  transfers between devices with their start and end apart: 18, of which 8 were waited for; matrix products, arithmetic and copies ran while one was open for 1% of the time, Pallas kernels for 6%

profile of v3, /device:TPU:1, one launch (start us, length us, event | category | flops | bytes accessed | tf_op | source)
XLA Modules:
  0.0 100.1 jit_solution(3023152813572776586)
XLA Ops:
  0.6 0.1 pad_add_fusion.pos
  0.7 1.0 %copy-done = bf16[1024,256]{1,0:T(8,128)(2,1)S(1)} copy-done((bf16[1024,256]{1,0:T(8,128)(2,1)S(1)}, bf16[1024,256]{1,0:T(8,128)(2,1)}, u32[]{:S(2)}) %copy-start) | copy-done | bytes 524312
  1.8 0.7 copy-done.3
  2.4 0.7 mask.1
  3.2 3.3 %collective-permute-start = (bf16[2,256,256]{2,1,0:T(8,128)(2,1)S(1)}, bf16[2,256,256]{2,1,0:T(8,128)(2,1)S(1)}, u32[]{:S(2)}, u32[]{:S(2)}) collective-permute-start(bf16[2,256,256]{2,1,0:T(8,128)(2,1)S(1)} %get-tuple-element.12), channel_id=1, source_target_pairs={{0,1},{1,0},{2,3},{3,2},{4,5},{5,4},{6,7},{7,6},{8,9},{9,8},{10,11... | collective-permute-start | bytes 786440 | tf_op jit(solution)/shard_map/ppermute | solution.py:218
  6.5 0.0 collective-permute-start.4
  6.5 2.7 %collective-permute-start.5 = (bf16[1024,256]{1,0:T(8,128)(2,1)S(1)}, bf16[1024,256]{1,0:T(8,128)(2,1)S(1)}, u32[]{:S(2)}, u32[]{:S(2)}) collective-permute-start(bf16[1024,256]{1,0:T(8,128)(2,1)S(1)} %get-tuple-element.13.m), channel_id=1, source_target_pairs={{0,6},{1,25},{2,0},{3,27},{4,2},{5,29},{6,4},{7,31},{8,14},{9,1},{... | collective-permute-start | bytes 1572872 | tf_op jit(solution)/shard_map/ppermute | solution.py:41
  9.2 0.0 collective-permute-start.6
  9.2 0.0 collective-permute-done
  9.3 5.6 %collective-permute-start.8 = (bf16[4,256,256]{2,1,0:T(8,128)(2,1)S(1)}, bf16[4,256,256]{2,1,0:T(8,128)(2,1)S(1)}, u32[]{:S(2)}, u32[]{:S(2)}) collective-permute-start(bf16[4,256,256]{2,1,0:T(8,128)(2,1)S(1)} %constant_dynamic-update-slice_fusion.refs_0_), channel_id=1, source_target_pairs={{0,224},{32,0},{64,32},{96,64},{128,96},{160,128},{192,160},{224,1... | collective-permute-start | bytes 1572872 | tf_op jit(solution)/shard_map/ppermute | solution.py:27
  14.9 0.1 collective-permute-start.1
  15.0 6.7 %collective-permute-done.4 = bf16[1024,256]{1,0:T(8,128)(2,1)S(1)} collective-permute-done((bf16[1024,256]{1,0:T(8,128)(2,1)S(1)}, bf16[1024,256]{1,0:T(8,128)(2,1)S(1)}, u32[]{:S(2)}, u32[]{:S(2)}) %collective-permute-start.4) | collective-permute-done | bytes 524320 | tf_op jit(solution)/shard_map/ppermute | solution.py:41
  21.7 0.0 collective-permute-done.5
  21.8 0.0 collective-permute-done.6
  21.8 1.8 %collective-permute-start.11 = (bf16[4096,256]{1,0:T(8,128)(2,1)S(1)}, bf16[4096,256]{1,0:T(8,128)(2,1)S(1)}, u32[]{:S(2)}, u32[]{:S(2)}) collective-permute-start(bf16[4096,256]{1,0:T(8,128)(2,1)S(1)} %constant_dynamic-update-slice_fusion.2.line), channel_id=1, source_target_pairs={{0,24},{1,7},{2,26},{3,1},{4,28},{5,3},{6,30},{7,5},{8,0},{9,15},{... | collective-permute-start | bytes 6291464 | tf_op jit(solution)/shard_map/ppermute | solution.py:41
  23.7 0.0 collective-permute-start.7
  23.7 1.7 %collective-permute-done.8.x = bf16[4,256,256]{2,1,0:T(8,128)(2,1)S(1)} collective-permute-done((bf16[4,256,256]{2,1,0:T(8,128)(2,1)S(1)}, bf16[4,256,256]{2,1,0:T(8,128)(2,1)S(1)}, u32[]{:S(2)}, u32[]{:S(2)}) %collective-permute-start.8) | collective-permute-done | bytes 524320 | tf_op jit(solution)/shard_map/ppermute | solution.py:27
  25.4 3.7 %collective-permute-start.9 = (bf16[4,256,256]{2,1,0:T(8,128)(2,1)S(1)}, bf16[4,256,256]{2,1,0:T(8,128)(2,1)S(1)}, u32[]{:S(2)}, u32[]{:S(2)}) collective-permute-start(bf16[4,256,256]{2,1,0:T(8,128)(2,1)S(1)} %hold.9.refs_4_), channel_id=1, source_target_pairs={{0,224},{32,0},{64,32},{96,64},{128,96},{160,128},{192,160},{224,1... | collective-permute-start | bytes 1572872 | tf_op jit(solution)/shard_map/ppermute | solution.py:27
  29.1 0.0 collective-permute-done.1.x
  29.1 0.0 collective-permute-start.2
  29.1 9.7 %collective-permute-done.9.x = bf16[4,256,256]{2,1,0:T(8,128)(2,1)S(1)} collective-permute-done((bf16[4,256,256]{2,1,0:T(8,128)(2,1)S(1)}, bf16[4,256,256]{2,1,0:T(8,128)(2,1)S(1)}, u32[]{:S(2)}, u32[]{:S(2)}) %collective-permute-start.9) | collective-permute-done | bytes 524320 | tf_op jit(solution)/shard_map/ppermute | solution.py:27
  38.8 3.4 %collective-permute-start.10 = (bf16[4,256,256]{2,1,0:T(8,128)(2,1)S(1)}, bf16[4,256,256]{2,1,0:T(8,128)(2,1)S(1)}, u32[]{:S(2)}, u32[]{:S(2)}) collective-permute-start(bf16[4,256,256]{2,1,0:T(8,128)(2,1)S(1)} %hold.10.refs_5_), channel_id=1, source_target_pairs={{0,224},{32,0},{64,32},{96,64},{128,96},{160,128},{192,160},{224,1... | collective-permute-start | bytes 1572872 | tf_op jit(solution)/shard_map/ppermute | solution.py:27
  42.2 0.0 collective-permute-done.2.x
  42.2 0.0 collective-permute-start.3
  42.2 7.9 %collective-permute-done.7.line_p = bf16[4096,256]{1,0:T(8,128)(2,1)S(1)} collective-permute-done((bf16[4096,256]{1,0:T(8,128)(2,1)S(1)}, bf16[4096,256]{1,0:T(8,128)(2,1)S(1)}, u32[]{:S(2)}, u32[]{:S(2)}) %collective-permute-start.7) | collective-permute-done | bytes 2097184 | tf_op jit(solution)/shard_map/ppermute | solution.py:41
  50.0 0.1 slice.32
  50.1 0.1 collective-permute-start.14
  50.2 0.0 collective-permute-done.11.line_m
  50.2 0.1 slice.33
  50.3 2.7 %collective-permute-start.15 = (bf16[2048,256]{1,0:T(8,128)(2,1)S(1)}, bf16[2048,256]{1,0:T(8,128)(2,1)S(1)}, u32[]{:S(2)}, u32[]{:S(2)}) collective-permute-start(bf16[2048,256]{1,0:T(8,128)(2,1)S(1)} %slice.33), channel_id=1, source_target_pairs={{0,24},{1,7},{2,26},{3,1},{4,28},{5,3},{6,30},{7,5},{8,0},{9,15},{... | collective-permute-start | bytes 3145736 | tf_op jit(solution)/shard_map/ppermute | solution.py:41
  53.0 0.0 collective-permute-done.10.x
  53.0 1.0 %collective-permute-done.3.x = bf16[4,256,256]{2,1,0:T(8,128)(2,1)S(1)} collective-permute-done((bf16[4,256,256]{2,1,0:T(8,128)(2,1)S(1)}, bf16[4,256,256]{2,1,0:T(8,128)(2,1)S(1)}, u32[]{:S(2)}, u32[]{:S(2)}) %collective-permute-start.3) | collective-permute-done | bytes 524320 | tf_op jit(solution)/shard_map/ppermute | solution.py:27
  54.1 4.4 %collective-permute-start.13 = (bf16[2,256,256]{2,1,0:T(8,128)(2,1)S(1)}, bf16[2,256,256]{2,1,0:T(8,128)(2,1)S(1)}, u32[]{:S(2)}, u32[]{:S(2)}) collective-permute-start(bf16[2,256,256]{2,1,0:T(8,128)(2,1)S(1)} %slice.25), channel_id=1, source_target_pairs={{0,224},{32,0},{64,32},{96,64},{128,96},{160,128},{192,160},{224,1... | collective-permute-start | bytes 786440 | tf_op jit(solution)/shard_map/ppermute | solution.py:27
  58.6 0.3 collective-permute-start.12
  58.8 3.0 %collective-permute-done.13.refs_8_ = bf16[2,256,256]{2,1,0:T(8,128)(2,1)S(1)} collective-permute-done((bf16[2,256,256]{2,1,0:T(8,128)(2,1)S(1)}, bf16[2,256,256]{2,1,0:T(8,128)(2,1)S(1)}, u32[]{:S(2)}, u32[]{:S(2)}) %collective-permute-start.13) | collective-permute-done | bytes 262176 | tf_op jit(solution)/shard_map/ppermute | solution.py:27
  61.9 3.7 %collective-permute-done.12.refs_7_ = bf16[2,256,256]{2,1,0:T(8,128)(2,1)S(1)} collective-permute-done((bf16[2,256,256]{2,1,0:T(8,128)(2,1)S(1)}, bf16[2,256,256]{2,1,0:T(8,128)(2,1)S(1)}, u32[]{:S(2)}, u32[]{:S(2)}) %collective-permute-start.12) | collective-permute-done | bytes 262176 | tf_op jit(solution)/shard_map/ppermute | solution.py:27
  65.5 0.9 rows.1.b
  66.5 0.0 copy-start.1
  66.5 0.0 copy-start.2
  66.5 3.9 %near.1 = (f32[1024,256]{1,0:T(8,128)S(1)}, f32[1024,256]{1,0:T(8,128)S(1)}) custom-call(bf16[2,4096,256]{2,1,0:T(8,128)(2,1)S(1)} %rows.1.b, bf16[4096,256]{1,0:T(8,128)(2,1)S(1)} %constant_dynamic-update-slice_fusion.2.line, bf16[4096,256]{1,0:T(8,128)(2,1)S(1)} %collective-permute-done.7.line_p, bf16[4096,256]{1,0:T(8,128)(2,1)S(1)} %collective-permute-done.11.line_m), custom_call_target="tpu_custom_call" | custom-call | flops 3200000000 | bytes 12000000 | tf_op jit(solution)/shard_map/near/pallas_call | solution.py:235
  70.4 1.6 %far_peer.1 = (f32[1024,256]{1,0:T(8,128)S(1)}, f32[1,128]{1,0:T(1,128)S(1)}) custom-call(s32[4]{0:T(128)S(1)} %pad_add_fusion.pos, s32[2,8]{1,0:T(2,128)S(1)} %bitcast.10, s32[8]{0:T(128)S(1)} %copy-done.2, bf16[1024,256]{1,0:T(8,128)(2,1)S(1)} %get-tuple-element.13.m, bf16[2,4096,256]{2,1,0:T(8,128)(2,1)S(1)} %rows.1.b, ...), custom_call_target="tpu_custom_call" | custom-call | flops 540000000 | bytes 4000000 | tf_op jit(solution)/shard_map/far_peer/pallas_call | solution.py:245
  72.1 4.1 %collective-permute-start.16 = (f32[1024,256]{1,0:T(8,128)S(1)}, f32[1024,256]{1,0:T(8,128)S(1)}, u32[]{:S(2)}, u32[]{:S(2)}) collective-permute-start(f32[1024,256]{1,0:T(8,128)S(1)} %get-tuple-element.19), channel_id=1, source_target_pairs={{0,1},{1,0},{2,3},{3,2},{4,5},{5,4},{6,7},{7,6},{8,9},{9,8},{10,11... | collective-permute-start | bytes 3145736 | tf_op jit(solution)/shard_map/ppermute | solution.py:263
  76.2 19.1 %all_to_all.5 = f32[128,1,128]{2,1,0:T(1,128)S(1)} all-to-all(f32[128,1,128]{2,1,0:T(1,128)S(1)} %broadcast_in_dim.9), channel_id=1, replica_groups=mesh['row'=8,'col_0'=4,'col_1'=4,'layer'=2] {'row','col_0','col_1'}, dimensions={0} | all-to-all | bytes 131072 | tf_op jit(solution)/shard_map/all_to_all | solution.py:201
  95.4 1.5 %collective-permute-start.17 = (f32[8,128]{1,0:T(8,128)S(1)}, f32[8,128]{1,0:T(8,128)S(1)}, u32[]{:S(2)}, u32[]{:S(2)}) collective-permute-start(f32[8,128]{1,0:T(8,128)S(1)} %bitcast_reduce_fusion), channel_id=1, source_target_pairs={{0,1},{1,0},{2,3},{3,2},{4,5},{5,4},{6,7},{7,6},{8,9},{9,8},{10,11... | collective-permute-start | bytes 12296 | tf_op jit(solution)/shard_map/ppermute | solution.py:202
  96.9 0.7 far_own.1.own
  97.6 0.1 collective-permute-done.17
  97.7 0.7 fusion.1
  98.4 1.8 %final.1 = f32[1024,256]{1,0:T(8,128)} custom-call(s32[2,8]{1,0:T(2,128)S(1)} %bitcast.11, s32[8]{0:T(128)S(1)} %copy-done.2, f32[1024,256]{1,0:T(8,128)S(1)} %far_own.1.own, f32[1024,256]{1,0:T(8,128)S(1)} %collective-permute-done.16.recv, bf16[1024,256]{1,0:T(8,128)(2,1)S(1)} %get-tuple-element.13.m), custom_call_target="tpu_custom_call" | custom-call | flops 2000000 | bytes 4000000 | tf_op jit(solution)/shard_map/final/pallas_call | solution.py:264
  (24 shorter events, 0.3 us)
Async XLA Ops:
  0.7 1.0 %copy-start = (bf16[1024,256]{1,0:T(8,128)(2,1)S(1)}, bf16[1024,256]{1,0:T(8,128)(2,1)}, u32[]{:S(2)}) copy-start(bf16[1024,256]{1,0:T(8,128)(2,1)} %x.1) | copy-start | bytes 1572868
  1.8 0.7 copy-start.3
  3.2 6.0 %collective-permute-start = (bf16[2,256,256]{2,1,0:T(8,128)(2,1)S(1)}, bf16[2,256,256]{2,1,0:T(8,128)(2,1)S(1)}, u32[]{:S(2)}, u32[]{:S(2)}) collective-permute-start(bf16[2,256,256]{2,1,0:T(8,128)(2,1)S(1)} %get-tuple-element.12), channel_id=1, source_target_pairs={{0,1},{1,0},{2,3},{3,2},{4,5},{5,4},{6,7},{7,6},{8,9},{9,8},{10,11... | collective-permute-start | bytes 786440 | tf_op jit(solution)/shard_map/ppermute | solution.py:218
  6.5 15.2 %collective-permute-start.4 = (bf16[1024,256]{1,0:T(8,128)(2,1)S(1)}, bf16[1024,256]{1,0:T(8,128)(2,1)S(1)}, u32[]{:S(2)}, u32[]{:S(2)}) collective-permute-start(bf16[1024,256]{1,0:T(8,128)(2,1)S(1)} %get-tuple-element.13.m), channel_id=1, source_target_pairs={{0,2},{1,9},{2,4},{3,11},{4,6},{5,13},{6,0},{7,15},{8,10},{9,17},{... | collective-permute-start | bytes 1572872 | tf_op jit(solution)/shard_map/ppermute | solution.py:41
  6.5 15.2 %collective-permute-start.5 = (bf16[1024,256]{1,0:T(8,128)(2,1)S(1)}, bf16[1024,256]{1,0:T(8,128)(2,1)S(1)}, u32[]{:S(2)}, u32[]{:S(2)}) collective-permute-start(bf16[1024,256]{1,0:T(8,128)(2,1)S(1)} %get-tuple-element.13.m), channel_id=1, source_target_pairs={{0,6},{1,25},{2,0},{3,27},{4,2},{5,29},{6,4},{7,31},{8,14},{9,1},{... | collective-permute-start | bytes 1572872 | tf_op jit(solution)/shard_map/ppermute | solution.py:41
  9.2 12.6 %collective-permute-start.6 = (bf16[1024,256]{1,0:T(8,128)(2,1)S(1)}, bf16[1024,256]{1,0:T(8,128)(2,1)S(1)}, u32[]{:S(2)}, u32[]{:S(2)}) collective-permute-start(bf16[1024,256]{1,0:T(8,128)(2,1)S(1)} %get-tuple-element.13.m), channel_id=1, source_target_pairs={{0,4},{1,17},{2,6},{3,19},{4,0},{5,21},{6,2},{7,23},{8,12},{9,25},... | collective-permute-start | bytes 1572872 | tf_op jit(solution)/shard_map/ppermute | solution.py:41
  9.3 16.1 %collective-permute-start.8 = (bf16[4,256,256]{2,1,0:T(8,128)(2,1)S(1)}, bf16[4,256,256]{2,1,0:T(8,128)(2,1)S(1)}, u32[]{:S(2)}, u32[]{:S(2)}) collective-permute-start(bf16[4,256,256]{2,1,0:T(8,128)(2,1)S(1)} %constant_dynamic-update-slice_fusion.refs_0_), channel_id=1, source_target_pairs={{0,224},{32,0},{64,32},{96,64},{128,96},{160,128},{192,160},{224,1... | collective-permute-start | bytes 1572872 | tf_op jit(solution)/shard_map/ppermute | solution.py:27
  14.9 14.2 %collective-permute-start.1 = (bf16[4,256,256]{2,1,0:T(8,128)(2,1)S(1)}, bf16[4,256,256]{2,1,0:T(8,128)(2,1)S(1)}, u32[]{:S(2)}, u32[]{:S(2)}) collective-permute-start(bf16[4,256,256]{2,1,0:T(8,128)(2,1)S(1)} %constant_dynamic-update-slice_fusion.refs_0_), channel_id=1, source_target_pairs={{0,32},{32,64},{64,96},{96,128},{128,160},{160,192},{192,224},{224... | collective-permute-start | bytes 1572872 | tf_op jit(solution)/shard_map/ppermute | solution.py:27
  21.8 28.4 %collective-permute-start.11 = (bf16[4096,256]{1,0:T(8,128)(2,1)S(1)}, bf16[4096,256]{1,0:T(8,128)(2,1)S(1)}, u32[]{:S(2)}, u32[]{:S(2)}) collective-permute-start(bf16[4096,256]{1,0:T(8,128)(2,1)S(1)} %constant_dynamic-update-slice_fusion.2.line), channel_id=1, source_target_pairs={{0,24},{1,7},{2,26},{3,1},{4,28},{5,3},{6,30},{7,5},{8,0},{9,15},{... | collective-permute-start | bytes 6291464 | tf_op jit(solution)/shard_map/ppermute | solution.py:41
  23.7 26.4 %collective-permute-start.7 = (bf16[4096,256]{1,0:T(8,128)(2,1)S(1)}, bf16[4096,256]{1,0:T(8,128)(2,1)S(1)}, u32[]{:S(2)}, u32[]{:S(2)}) collective-permute-start(bf16[4096,256]{1,0:T(8,128)(2,1)S(1)} %constant_dynamic-update-slice_fusion.2.line), channel_id=1, source_target_pairs={{0,8},{1,3},{2,10},{3,5},{4,12},{5,7},{6,14},{7,1},{8,16},{9,11},{... | collective-permute-start | bytes 6291464 | tf_op jit(solution)/shard_map/ppermute | solution.py:41
  25.4 13.4 %collective-permute-start.9 = (bf16[4,256,256]{2,1,0:T(8,128)(2,1)S(1)}, bf16[4,256,256]{2,1,0:T(8,128)(2,1)S(1)}, u32[]{:S(2)}, u32[]{:S(2)}) collective-permute-start(bf16[4,256,256]{2,1,0:T(8,128)(2,1)S(1)} %hold.9.refs_4_), channel_id=1, source_target_pairs={{0,224},{32,0},{64,32},{96,64},{128,96},{160,128},{192,160},{224,1... | collective-permute-start | bytes 1572872 | tf_op jit(solution)/shard_map/ppermute | solution.py:27
  29.1 13.1 %collective-permute-start.2 = (bf16[4,256,256]{2,1,0:T(8,128)(2,1)S(1)}, bf16[4,256,256]{2,1,0:T(8,128)(2,1)S(1)}, u32[]{:S(2)}, u32[]{:S(2)}) collective-permute-start(bf16[4,256,256]{2,1,0:T(8,128)(2,1)S(1)} %hold.6.refs_1_), channel_id=1, source_target_pairs={{0,32},{32,64},{64,96},{96,128},{128,160},{160,192},{192,224},{224... | collective-permute-start | bytes 1572872 | tf_op jit(solution)/shard_map/ppermute | solution.py:27
  38.8 14.3 %collective-permute-start.10 = (bf16[4,256,256]{2,1,0:T(8,128)(2,1)S(1)}, bf16[4,256,256]{2,1,0:T(8,128)(2,1)S(1)}, u32[]{:S(2)}, u32[]{:S(2)}) collective-permute-start(bf16[4,256,256]{2,1,0:T(8,128)(2,1)S(1)} %hold.10.refs_5_), channel_id=1, source_target_pairs={{0,224},{32,0},{64,32},{96,64},{128,96},{160,128},{192,160},{224,1... | collective-permute-start | bytes 1572872 | tf_op jit(solution)/shard_map/ppermute | solution.py:27
  42.2 11.9 %collective-permute-start.3 = (bf16[4,256,256]{2,1,0:T(8,128)(2,1)S(1)}, bf16[4,256,256]{2,1,0:T(8,128)(2,1)S(1)}, u32[]{:S(2)}, u32[]{:S(2)}) collective-permute-start(bf16[4,256,256]{2,1,0:T(8,128)(2,1)S(1)} %hold.7.refs_2_), channel_id=1, source_target_pairs={{0,32},{32,64},{64,96},{96,128},{128,160},{160,192},{192,224},{224... | collective-permute-start | bytes 1572872 | tf_op jit(solution)/shard_map/ppermute | solution.py:27
  50.1 20.3 %collective-permute-start.14 = (bf16[2048,256]{1,0:T(8,128)(2,1)S(1)}, bf16[2048,256]{1,0:T(8,128)(2,1)S(1)}, u32[]{:S(2)}, u32[]{:S(2)}) collective-permute-start(bf16[2048,256]{1,0:T(8,128)(2,1)S(1)} %slice.32), channel_id=1, source_target_pairs={{0,8},{1,3},{2,10},{3,5},{4,12},{5,7},{6,14},{7,1},{8,16},{9,11},{... | collective-permute-start | bytes 3145736 | tf_op jit(solution)/shard_map/ppermute | solution.py:41
  50.3 20.1 %collective-permute-start.15 = (bf16[2048,256]{1,0:T(8,128)(2,1)S(1)}, bf16[2048,256]{1,0:T(8,128)(2,1)S(1)}, u32[]{:S(2)}, u32[]{:S(2)}) collective-permute-start(bf16[2048,256]{1,0:T(8,128)(2,1)S(1)} %slice.33), channel_id=1, source_target_pairs={{0,24},{1,7},{2,26},{3,1},{4,28},{5,3},{6,30},{7,5},{8,0},{9,15},{... | collective-permute-start | bytes 3145736 | tf_op jit(solution)/shard_map/ppermute | solution.py:41
  54.1 7.7 %collective-permute-start.13 = (bf16[2,256,256]{2,1,0:T(8,128)(2,1)S(1)}, bf16[2,256,256]{2,1,0:T(8,128)(2,1)S(1)}, u32[]{:S(2)}, u32[]{:S(2)}) collective-permute-start(bf16[2,256,256]{2,1,0:T(8,128)(2,1)S(1)} %slice.25), channel_id=1, source_target_pairs={{0,224},{32,0},{64,32},{96,64},{128,96},{160,128},{192,160},{224,1... | collective-permute-start | bytes 786440 | tf_op jit(solution)/shard_map/ppermute | solution.py:27
  58.6 7.0 %collective-permute-start.12 = (bf16[2,256,256]{2,1,0:T(8,128)(2,1)S(1)}, bf16[2,256,256]{2,1,0:T(8,128)(2,1)S(1)}, u32[]{:S(2)}, u32[]{:S(2)}) collective-permute-start(bf16[2,256,256]{2,1,0:T(8,128)(2,1)S(1)} %slice.24), channel_id=1, source_target_pairs={{0,32},{32,64},{64,96},{96,128},{128,160},{160,192},{192,224},{224... | collective-permute-start | bytes 786440 | tf_op jit(solution)/shard_map/ppermute | solution.py:27
  66.5 4.0 %copy-start.1 = (s32[8,2]{0,1:T(2,128)S(1)}, s32[8,2]{0,1:T(2,128)}, u32[]{:S(2)}) copy-start(s32[8,2]{0,1:T(2,128)} %param.6) | copy-start | bytes 196
  66.5 4.0 %copy-start.2 = (s32[8]{0:T(128)S(1)}, s32[8]{0:T(128)}, u32[]{:S(2)}) copy-start(s32[8]{0:T(128)} %flag.3) | copy-start | bytes 100
  72.1 26.3 %collective-permute-start.16 = (f32[1024,256]{1,0:T(8,128)S(1)}, f32[1024,256]{1,0:T(8,128)S(1)}, u32[]{:S(2)}, u32[]{:S(2)}) collective-permute-start(f32[1024,256]{1,0:T(8,128)S(1)} %get-tuple-element.19), channel_id=1, source_target_pairs={{0,1},{1,0},{2,3},{3,2},{4,5},{5,4},{6,7},{7,6},{8,9},{9,8},{10,11... | collective-permute-start | bytes 3145736 | tf_op jit(solution)/shard_map/ppermute | solution.py:263
  95.4 2.3 %collective-permute-start.17 = (f32[8,128]{1,0:T(8,128)S(1)}, f32[8,128]{1,0:T(8,128)S(1)}, u32[]{:S(2)}, u32[]{:S(2)}) collective-permute-start(f32[8,128]{1,0:T(8,128)S(1)} %bitcast_reduce_fusion), channel_id=1, source_target_pairs={{0,1},{1,0},{2,3},{3,2},{4,5},{5,4},{6,7},{7,6},{8,9},{9,8},{10,11... | collective-permute-start | bytes 12296 | tf_op jit(solution)/shard_map/ppermute | solution.py:202

commit v4 on v3

--- a/solution.py
+++ b/solution.py
@@ -137,10 +137,6 @@
         rows = pl.ds(i * 256, 256)
         a = jnp.concatenate([(q0, q1)[k // 2][pl.ds((k % 2) * 1024 + i * 256, 256), :] for k in range(4)], axis=1)
         new[rows, :] = old[rows, :] + jnp.dot(a, b[ch, pl.ds(3072, 1024), :], preferred_element_type=jnp.float32)
-
-
-def far_own_kernel(b, q0, q1, p_own, tie, new):
-    far_rows(b, q0, q1, 0, p_own, new)
 
 
 def far_peer_kernel(pos, keep, flag, m, b, q0, q1, p_own, p_peer, new, out):
@@ -178,14 +174,19 @@
         out[...] = total
 
 
-def final_kernel(keep, flag, own, recv, m, out):
-    for i in range(8):
-        take = flag[i] == 1
-        sign, twice = jnp.where(take, 1.0, -1.0), jnp.where(take, 0.0, 2.0)
-        for j in range(2):
-            at = (pl.ds(i * BLK, BLK), pl.ds(j * BLK, BLK))
-            square = own[at] + recv[at]
-            out[at] = (twice * m[at].astype(jnp.float32) + sign * square) * keep[j, i].astype(jnp.float32)
+def final_kernel(keep, flag, b, q0, q1, p_own, recv, m, out):
+    for n in range(4):
+        rows = pl.ds(n * 256, 256)
+        a = jnp.concatenate([(q0, q1)[k // 2][pl.ds((k % 2) * 1024 + n * 256, 256), :] for k in range(4)], axis=1)
+        product = jnp.dot(a, b[0, pl.ds(3072, 1024), :], preferred_element_type=jnp.float32)
+        square = p_own[rows, :] + recv[rows, :] + product
+        for i in (2 * n, 2 * n + 1):
+            take = flag[i] == 1
+            sign, twice = jnp.where(take, 1.0, -1.0), jnp.where(take, 0.0, 2.0)
+            for j in range(2):
+                at = (pl.ds(i * BLK, BLK), pl.ds(j * BLK, BLK))
+                part = square[(i % 2) * BLK : (i % 2 + 1) * BLK, j * BLK : (j + 1) * BLK]
+                out[at] = (twice * m[at].astype(jnp.float32) + sign * part) * keep[j, i].astype(jnp.float32)
 
 
 def bf16(*shape):
@@ -196,10 +197,14 @@
     return jax.ShapeDtypeStruct(shape, jnp.float32)
 
 
-def trace_of(parts):
-    spread = jnp.broadcast_to(parts[None], (128, 1, BLK))
-    rows = lax.all_to_all(spread, ("row", Y, X), 0, 0).reshape(8, 16, BLK).sum(axis=1)
-    rows = rows + lax.ppermute(rows, "layer", [(0, 1), (1, 0)])
+def over_planes(parts):
+    spread = jnp.broadcast_to(parts[None], (64, 1, BLK))
+    planes = lax.all_to_all(spread, ("row", Y, "layer"), 0, 0).reshape(8, 8, BLK).sum(axis=1)
+    return [planes] + [lax.ppermute(planes, X, [(i, i ^ bits) for i in range(4)]) for bits in (1, 3, 2)]
+
+
+def trace_of(values):
+    rows = functools.reduce(jnp.add, values)
     square, keep, linear, branch = (rows[:, 8 * n : 8 * n + 8] for n in range(4))
     return jnp.sum(keep * jnp.where(branch == 1.0, square, 2.0 * linear - square))
 
@@ -251,26 +256,18 @@
         name="far_peer",
         cost_estimate=pl.CostEstimate(flops=540_000_000, bytes_accessed=4_000_000, transcendentals=0),
     )(pos, keep, branch_flag, m, inner, q0, q1, p_own, p_peer)
-    own_part = pl.pallas_call(
-        far_own_kernel,
-        out_shape=f32(1024, 256),
-        in_specs=[VMEM] * 5,
-        out_specs=VMEM,
-        compiler_params=room(10),
-        name="far_own",
-        cost_estimate=pl.CostEstimate(flops=540_000_000, bytes_accessed=4_000_000, transcendentals=0),
-    )(inner, q0, q1, p_own, parts)
     recv = lax.ppermute(peer_part, "layer", swap)
     updated = pl.pallas_call(
         final_kernel,
         out_shape=f32(1024, 256),
-        in_specs=[SMEM, SMEM, VMEM, VMEM, VMEM],
+        in_specs=[SMEM, SMEM] + [VMEM] * 6,
         out_specs=VMEM,
-        compiler_params=room(6),
+        compiler_params=room(12),
         name="final",
         cost_estimate=pl.CostEstimate(flops=2_000_000, bytes_accessed=4_000_000, transcendentals=0),
-    )(keep, branch_flag, own_part, recv, m)
-    return (updated, trace_of(parts))
+    )(keep, branch_flag, inner, q0, q1, p_own, recv, m)
+    updated, values = lax.optimization_barrier((updated, over_planes(parts)))
+    return (updated, trace_of(values))
 
 
 def solution(mesh):

time: 100 us -> 98.4 us (0.984)
  blocking collectives: 19.1 us -> 14.7 us
  starting transfers between devices: 33.8 us -> 35.6 us
    all_to_all x1, blocking collectives: 19.1 us -> 14.7 us  [over_planes(): lax.all_to_all(spread, ('row', Y, 'layer'), 0, 0).reshape(8, 8, BLK)]
    ppermute x1 -> x3, starting transfers between devices: 1.51 us -> 3.34 us  [over_planes(): lax.ppermute(planes, X, [(i, i ^ bits) for i in range(4)])]
  transfers between devices with their start and end apart: 18 -> 20, of which waited for: 8 -> 8; matrix products, arithmetic and copies ran while one was open for 1% -> 0% of each run, Pallas kernels for 6% -> 7%
where the time goes in v4:
time: 98.4 us; the launch traced here: 97.8 us
  starting transfers between devices  35.6 us (36%)
  waiting for transfers between devices  34.3 us (35%)
  blocking collectives  14.7 us (15%)
  Pallas kernels  9.51 us (10%)
  local copies, waits for them, and re-layouts  2.11 us (2%)
    ppermute x8, waiting for transfers between devices, shift(): return lax.ppermute(value, axis, [(i, (i + off) % n) for i in range(n)])  19.2 us
    ppermute x8, starting transfers between devices, shift(): return lax.ppermute(value, axis, [(i, (i + off) % n) for i in range(n)])  17.5 us
    all_to_all x1, blocking collectives, over_planes(): lax.all_to_all(spread, ('row', Y, 'layer'), 0, 0).reshape(8, 8, BLK)  14.7 us
    ppermute x7, waiting for transfers between devices, turn(): return lax.ppermute(value, ('row', Y, X, 'layer'), pairs)  14.6 us
    ppermute x7, starting transfers between devices, turn(): return lax.ppermute(value, ('row', Y, X, 'layer'), pairs)  7.33 us
    ppermute x1, starting transfers between devices, on_device(): recv = lax.ppermute(peer_part, 'layer', swap)  4.1 us
    pallas_call x1, Pallas kernels, on_device(): pl.pallas_call(near_kernel, out_shape=[f32(1024, 256), f32(1024, 256)], i...  3.9 us
    ppermute x3, starting transfers between devices, over_planes(): lax.ppermute(planes, X, [(i, i ^ bits) for i in range(4)])  3.34 us
  transfers between devices with their start and end apart: 20, of which 8 were waited for; matrix products, arithmetic and copies ran while one was open for 0% of the time, Pallas kernels for 7%

profile of v4, /device:TPU:1, one launch (start us, length us, event | category | flops | bytes accessed | tf_op | source)
XLA Modules:
  0.0 97.8 jit_solution(13400793991287308950)
XLA Ops:
  0.6 0.1 pad_add_fusion.pos
  0.7 1.0 %copy-done = bf16[1024,256]{1,0:T(8,128)(2,1)S(1)} copy-done((bf16[1024,256]{1,0:T(8,128)(2,1)S(1)}, bf16[1024,256]{1,0:T(8,128)(2,1)}, u32[]{:S(2)}) %copy-start) | copy-done | bytes 524312
  1.8 0.7 copy-done.3
  2.4 0.7 mask.1
  3.2 3.3 %collective-permute-start = (bf16[2,256,256]{2,1,0:T(8,128)(2,1)S(1)}, bf16[2,256,256]{2,1,0:T(8,128)(2,1)S(1)}, u32[]{:S(2)}, u32[]{:S(2)}) collective-permute-start(bf16[2,256,256]{2,1,0:T(8,128)(2,1)S(1)} %get-tuple-element.17), channel_id=1, source_target_pairs={{0,1},{1,0},{2,3},{3,2},{4,5},{5,4},{6,7},{7,6},{8,9},{9,8},{10,11... | collective-permute-start | bytes 786440 | tf_op jit(solution)/shard_map/ppermute | solution.py:223
  6.5 0.0 collective-permute-start.4
  6.5 2.7 %collective-permute-start.5 = (bf16[1024,256]{1,0:T(8,128)(2,1)S(1)}, bf16[1024,256]{1,0:T(8,128)(2,1)S(1)}, u32[]{:S(2)}, u32[]{:S(2)}) collective-permute-start(bf16[1024,256]{1,0:T(8,128)(2,1)S(1)} %get-tuple-element.18.m), channel_id=1, source_target_pairs={{0,6},{1,25},{2,0},{3,27},{4,2},{5,29},{6,4},{7,31},{8,14},{9,1},{... | collective-permute-start | bytes 1572872 | tf_op jit(solution)/shard_map/ppermute | solution.py:41
  9.2 0.0 collective-permute-start.6
  9.2 0.0 collective-permute-done
  9.3 5.6 %collective-permute-start.8 = (bf16[4,256,256]{2,1,0:T(8,128)(2,1)S(1)}, bf16[4,256,256]{2,1,0:T(8,128)(2,1)S(1)}, u32[]{:S(2)}, u32[]{:S(2)}) collective-permute-start(bf16[4,256,256]{2,1,0:T(8,128)(2,1)S(1)} %constant_dynamic-update-slice_fusion.refs_0_), channel_id=1, source_target_pairs={{0,224},{32,0},{64,32},{96,64},{128,96},{160,128},{192,160},{224,1... | collective-permute-start | bytes 1572872 | tf_op jit(solution)/shard_map/ppermute | solution.py:27
  14.9 0.1 collective-permute-start.1
  15.0 6.7 %collective-permute-done.4 = bf16[1024,256]{1,0:T(8,128)(2,1)S(1)} collective-permute-done((bf16[1024,256]{1,0:T(8,128)(2,1)S(1)}, bf16[1024,256]{1,0:T(8,128)(2,1)S(1)}, u32[]{:S(2)}, u32[]{:S(2)}) %collective-permute-start.4) | collective-permute-done | bytes 524320 | tf_op jit(solution)/shard_map/ppermute | solution.py:41
  21.7 0.0 collective-permute-done.5
  21.8 0.0 collective-permute-done.6
  21.8 1.8 %collective-permute-start.11 = (bf16[4096,256]{1,0:T(8,128)(2,1)S(1)}, bf16[4096,256]{1,0:T(8,128)(2,1)S(1)}, u32[]{:S(2)}, u32[]{:S(2)}) collective-permute-start(bf16[4096,256]{1,0:T(8,128)(2,1)S(1)} %constant_dynamic-update-slice_fusion.2.line), channel_id=1, source_target_pairs={{0,24},{1,7},{2,26},{3,1},{4,28},{5,3},{6,30},{7,5},{8,0},{9,15},{... | collective-permute-start | bytes 6291464 | tf_op jit(solution)/shard_map/ppermute | solution.py:41
  23.7 0.0 collective-permute-start.7
  23.7 1.7 %collective-permute-done.8.x = bf16[4,256,256]{2,1,0:T(8,128)(2,1)S(1)} collective-permute-done((bf16[4,256,256]{2,1,0:T(8,128)(2,1)S(1)}, bf16[4,256,256]{2,1,0:T(8,128)(2,1)S(1)}, u32[]{:S(2)}, u32[]{:S(2)}) %collective-permute-start.8) | collective-permute-done | bytes 524320 | tf_op jit(solution)/shard_map/ppermute | solution.py:27
  25.4 3.7 %collective-permute-start.9 = (bf16[4,256,256]{2,1,0:T(8,128)(2,1)S(1)}, bf16[4,256,256]{2,1,0:T(8,128)(2,1)S(1)}, u32[]{:S(2)}, u32[]{:S(2)}) collective-permute-start(bf16[4,256,256]{2,1,0:T(8,128)(2,1)S(1)} %hold.9.refs_4_), channel_id=1, source_target_pairs={{0,224},{32,0},{64,32},{96,64},{128,96},{160,128},{192,160},{224,1... | collective-permute-start | bytes 1572872 | tf_op jit(solution)/shard_map/ppermute | solution.py:27
  29.1 0.0 collective-permute-start.2
  29.1 9.7 %collective-permute-done.9.x = bf16[4,256,256]{2,1,0:T(8,128)(2,1)S(1)} collective-permute-done((bf16[4,256,256]{2,1,0:T(8,128)(2,1)S(1)}, bf16[4,256,256]{2,1,0:T(8,128)(2,1)S(1)}, u32[]{:S(2)}, u32[]{:S(2)}) %collective-permute-start.9) | collective-permute-done | bytes 524320 | tf_op jit(solution)/shard_map/ppermute | solution.py:27
  38.8 3.4 %collective-permute-start.10 = (bf16[4,256,256]{2,1,0:T(8,128)(2,1)S(1)}, bf16[4,256,256]{2,1,0:T(8,128)(2,1)S(1)}, u32[]{:S(2)}, u32[]{:S(2)}) collective-permute-start(bf16[4,256,256]{2,1,0:T(8,128)(2,1)S(1)} %hold.10.refs_5_), channel_id=1, source_target_pairs={{0,224},{32,0},{64,32},{96,64},{128,96},{160,128},{192,160},{224,1... | collective-permute-start | bytes 1572872 | tf_op jit(solution)/shard_map/ppermute | solution.py:27
  42.2 0.0 collective-permute-start.3
  42.2 7.9 %collective-permute-done.7.line_p = bf16[4096,256]{1,0:T(8,128)(2,1)S(1)} collective-permute-done((bf16[4096,256]{1,0:T(8,128)(2,1)S(1)}, bf16[4096,256]{1,0:T(8,128)(2,1)S(1)}, u32[]{:S(2)}, u32[]{:S(2)}) %collective-permute-start.7) | collective-permute-done | bytes 2097184 | tf_op jit(solution)/shard_map/ppermute | solution.py:41
  50.0 0.1 slice.32
  50.1 0.1 collective-permute-start.14
  50.2 0.0 collective-permute-done.11.line_m
  50.2 0.1 slice.33
  50.3 2.7 %collective-permute-start.15 = (bf16[2048,256]{1,0:T(8,128)(2,1)S(1)}, bf16[2048,256]{1,0:T(8,128)(2,1)S(1)}, u32[]{:S(2)}, u32[]{:S(2)}) collective-permute-start(bf16[2048,256]{1,0:T(8,128)(2,1)S(1)} %slice.33), channel_id=1, source_target_pairs={{0,24},{1,7},{2,26},{3,1},{4,28},{5,3},{6,30},{7,5},{8,0},{9,15},{... | collective-permute-start | bytes 3145736 | tf_op jit(solution)/shard_map/ppermute | solution.py:41
  53.0 1.0 %collective-permute-done.3.x = bf16[4,256,256]{2,1,0:T(8,128)(2,1)S(1)} collective-permute-done((bf16[4,256,256]{2,1,0:T(8,128)(2,1)S(1)}, bf16[4,256,256]{2,1,0:T(8,128)(2,1)S(1)}, u32[]{:S(2)}, u32[]{:S(2)}) %collective-permute-start.3) | collective-permute-done | bytes 524320 | tf_op jit(solution)/shard_map/ppermute | solution.py:27
  54.1 4.4 %collective-permute-start.13 = (bf16[2,256,256]{2,1,0:T(8,128)(2,1)S(1)}, bf16[2,256,256]{2,1,0:T(8,128)(2,1)S(1)}, u32[]{:S(2)}, u32[]{:S(2)}) collective-permute-start(bf16[2,256,256]{2,1,0:T(8,128)(2,1)S(1)} %slice.25), channel_id=1, source_target_pairs={{0,224},{32,0},{64,32},{96,64},{128,96},{160,128},{192,160},{224,1... | collective-permute-start | bytes 786440 | tf_op jit(solution)/shard_map/ppermute | solution.py:27
  58.6 0.3 collective-permute-start.12
  58.8 3.0 %collective-permute-done.13.refs_8_ = bf16[2,256,256]{2,1,0:T(8,128)(2,1)S(1)} collective-permute-done((bf16[2,256,256]{2,1,0:T(8,128)(2,1)S(1)}, bf16[2,256,256]{2,1,0:T(8,128)(2,1)S(1)}, u32[]{:S(2)}, u32[]{:S(2)}) %collective-permute-start.13) | collective-permute-done | bytes 262176 | tf_op jit(solution)/shard_map/ppermute | solution.py:27
  61.9 3.7 %collective-permute-done.12.refs_7_ = bf16[2,256,256]{2,1,0:T(8,128)(2,1)S(1)} collective-permute-done((bf16[2,256,256]{2,1,0:T(8,128)(2,1)S(1)}, bf16[2,256,256]{2,1,0:T(8,128)(2,1)S(1)}, u32[]{:S(2)}, u32[]{:S(2)}) %collective-permute-start.12) | collective-permute-done | bytes 262176 | tf_op jit(solution)/shard_map/ppermute | solution.py:27
  65.5 0.9 rows.1.b
  66.5 0.0 copy-start.1
  66.5 0.0 copy-start.2
  66.5 3.9 %near.1 = (f32[1024,256]{1,0:T(8,128)S(1)}, f32[1024,256]{1,0:T(8,128)S(1)}) custom-call(bf16[2,4096,256]{2,1,0:T(8,128)(2,1)S(1)} %rows.1.b, bf16[4096,256]{1,0:T(8,128)(2,1)S(1)} %constant_dynamic-update-slice_fusion.2.line, bf16[4096,256]{1,0:T(8,128)(2,1)S(1)} %collective-permute-done.7.line_p, bf16[4096,256]{1,0:T(8,128)(2,1)S(1)} %collective-permute-done.11.line_m), custom_call_target="tpu_custom_call" | custom-call | flops 3200000000 | bytes 12000000 | tf_op jit(solution)/shard_map/near/pallas_call | solution.py:240
  70.4 0.0 collective-permute-done.14.q0
  70.4 1.6 %far_peer.1 = (f32[1024,256]{1,0:T(8,128)S(1)}, f32[1,128]{1,0:T(1,128)S(1)}) custom-call(s32[4]{0:T(128)S(1)} %pad_add_fusion.pos, s32[2,8]{1,0:T(2,128)S(1)} %bitcast.10, s32[8]{0:T(128)S(1)} %copy-done.2, bf16[1024,256]{1,0:T(8,128)(2,1)S(1)} %get-tuple-element.18.m, bf16[2,4096,256]{2,1,0:T(8,128)(2,1)S(1)} %rows.1.b, ...), custom_call_target="tpu_custom_call" | custom-call | flops 540000000 | bytes 4000000 | tf_op jit(solution)/shard_map/far_peer/pallas_call | solution.py:250
  72.1 4.1 %collective-permute-start.16 = (f32[1024,256]{1,0:T(8,128)S(1)}, f32[1024,256]{1,0:T(8,128)S(1)}, u32[]{:S(2)}, u32[]{:S(2)}) collective-permute-start(f32[1024,256]{1,0:T(8,128)S(1)} %get-tuple-element.23), channel_id=1, source_target_pairs={{0,1},{1,0},{2,3},{3,2},{4,5},{5,4},{6,7},{7,6},{8,9},{9,8},{10,11... | collective-permute-start | bytes 3145736 | tf_op jit(solution)/shard_map/ppermute | solution.py:259
  76.2 14.7 %all_to_all.5 = f32[64,1,128]{2,1,0:T(1,128)S(1)} all-to-all(f32[64,1,128]{2,1,0:T(1,128)S(1)} %broadcast_in_dim.9), channel_id=1, replica_groups=mesh['row'=8,'col_0'=4,'col_1'=4,'layer'=2] {'row','col_0','layer'}, dimensions={0} | all-to-all | bytes 65536 | tf_op jit(solution)/shard_map/all_to_all | solution.py:202
  90.9 1.2 %collective-permute-start.17 = (f32[8,128]{1,0:T(8,128)S(1)}, f32[8,128]{1,0:T(8,128)S(1)}, u32[]{:S(2)}, u32[]{:S(2)}) collective-permute-start(f32[8,128]{1,0:T(8,128)S(1)} %bitcast_reduce_fusion), channel_id=1, source_target_pairs={{0,2},{2,0},{4,6},{6,4},{1,3},{3,1},{5,7},{7,5},{8,10},{10,8},{12,... | collective-permute-start | bytes 12296 | tf_op jit(solution)/shard_map/ppermute | solution.py:203
  92.2 1.0 %collective-permute-start.18 = (f32[8,128]{1,0:T(8,128)S(1)}, f32[8,128]{1,0:T(8,128)S(1)}, u32[]{:S(2)}, u32[]{:S(2)}) collective-permute-start(f32[8,128]{1,0:T(8,128)S(1)} %bitcast_reduce_fusion), channel_id=1, source_target_pairs={{0,6},{2,4},{4,2},{6,0},{1,7},{3,5},{5,3},{7,1},{8,14},{10,12},{12... | collective-permute-start | bytes 12296 | tf_op jit(solution)/shard_map/ppermute | solution.py:203
  93.2 1.1 %collective-permute-start.19 = (f32[8,128]{1,0:T(8,128)S(1)}, f32[8,128]{1,0:T(8,128)S(1)}, u32[]{:S(2)}, u32[]{:S(2)}) collective-permute-start(f32[8,128]{1,0:T(8,128)S(1)} %bitcast_reduce_fusion), channel_id=1, source_target_pairs={{0,4},{2,6},{4,0},{6,2},{1,5},{3,7},{5,1},{7,3},{8,12},{10,14},{12... | collective-permute-start | bytes 12296 | tf_op jit(solution)/shard_map/ppermute | solution.py:203
  94.3 2.3 %final.1 = f32[1024,256]{1,0:T(8,128)} custom-call(s32[2,8]{1,0:T(2,128)S(1)} %bitcast.11, s32[8]{0:T(128)S(1)} %copy-done.2, bf16[2,4096,256]{2,1,0:T(8,128)(2,1)S(1)} %rows.1.b, bf16[2048,256]{1,0:T(8,128)(2,1)S(1)} %collective-permute-done.14.q0, bf16[2048,256]{1,0:T(8,128)(2,1)S(1)} %collective-permute-done.15.q1, ...), custom_call_target="tpu_custom_call" | custom-call | flops 2000000 | bytes 4000000 | tf_op jit(solution)/shard_map/final/pallas_call | solution.py:260
  96.6 0.0 collective-permute-done.17
  96.6 0.5 collective-permute-done.19
  97.1 0.7 fusion.1
  (27 shorter events, 0.3 us)
Async XLA Ops:
  0.7 1.0 %copy-start = (bf16[1024,256]{1,0:T(8,128)(2,1)S(1)}, bf16[1024,256]{1,0:T(8,128)(2,1)}, u32[]{:S(2)}) copy-start(bf16[1024,256]{1,0:T(8,128)(2,1)} %x.1) | copy-start | bytes 1572868
  1.8 0.7 copy-start.3
  3.2 6.0 %collective-permute-start = (bf16[2,256,256]{2,1,0:T(8,128)(2,1)S(1)}, bf16[2,256,256]{2,1,0:T(8,128)(2,1)S(1)}, u32[]{:S(2)}, u32[]{:S(2)}) collective-permute-start(bf16[2,256,256]{2,1,0:T(8,128)(2,1)S(1)} %get-tuple-element.17), channel_id=1, source_target_pairs={{0,1},{1,0},{2,3},{3,2},{4,5},{5,4},{6,7},{7,6},{8,9},{9,8},{10,11... | collective-permute-start | bytes 786440 | tf_op jit(solution)/shard_map/ppermute | solution.py:223
  6.5 15.2 %collective-permute-start.4 = (bf16[1024,256]{1,0:T(8,128)(2,1)S(1)}, bf16[1024,256]{1,0:T(8,128)(2,1)S(1)}, u32[]{:S(2)}, u32[]{:S(2)}) collective-permute-start(bf16[1024,256]{1,0:T(8,128)(2,1)S(1)} %get-tuple-element.18.m), channel_id=1, source_target_pairs={{0,2},{1,9},{2,4},{3,11},{4,6},{5,13},{6,0},{7,15},{8,10},{9,17},{... | collective-permute-start | bytes 1572872 | tf_op jit(solution)/shard_map/ppermute | solution.py:41
  6.5 15.2 %collective-permute-start.5 = (bf16[1024,256]{1,0:T(8,128)(2,1)S(1)}, bf16[1024,256]{1,0:T(8,128)(2,1)S(1)}, u32[]{:S(2)}, u32[]{:S(2)}) collective-permute-start(bf16[1024,256]{1,0:T(8,128)(2,1)S(1)} %get-tuple-element.18.m), channel_id=1, source_target_pairs={{0,6},{1,25},{2,0},{3,27},{4,2},{5,29},{6,4},{7,31},{8,14},{9,1},{... | collective-permute-start | bytes 1572872 | tf_op jit(solution)/shard_map/ppermute | solution.py:41
  9.2 12.6 %collective-permute-start.6 = (bf16[1024,256]{1,0:T(8,128)(2,1)S(1)}, bf16[1024,256]{1,0:T(8,128)(2,1)S(1)}, u32[]{:S(2)}, u32[]{:S(2)}) collective-permute-start(bf16[1024,256]{1,0:T(8,128)(2,1)S(1)} %get-tuple-element.18.m), channel_id=1, source_target_pairs={{0,4},{1,17},{2,6},{3,19},{4,0},{5,21},{6,2},{7,23},{8,12},{9,25},... | collective-permute-start | bytes 1572872 | tf_op jit(solution)/shard_map/ppermute | solution.py:41
  9.3 16.1 %collective-permute-start.8 = (bf16[4,256,256]{2,1,0:T(8,128)(2,1)S(1)}, bf16[4,256,256]{2,1,0:T(8,128)(2,1)S(1)}, u32[]{:S(2)}, u32[]{:S(2)}) collective-permute-start(bf16[4,256,256]{2,1,0:T(8,128)(2,1)S(1)} %constant_dynamic-update-slice_fusion.refs_0_), channel_id=1, source_target_pairs={{0,224},{32,0},{64,32},{96,64},{128,96},{160,128},{192,160},{224,1... | collective-permute-start | bytes 1572872 | tf_op jit(solution)/shard_map/ppermute | solution.py:27
  14.9 14.2 %collective-permute-start.1 = (bf16[4,256,256]{2,1,0:T(8,128)(2,1)S(1)}, bf16[4,256,256]{2,1,0:T(8,128)(2,1)S(1)}, u32[]{:S(2)}, u32[]{:S(2)}) collective-permute-start(bf16[4,256,256]{2,1,0:T(8,128)(2,1)S(1)} %constant_dynamic-update-slice_fusion.refs_0_), channel_id=1, source_target_pairs={{0,32},{32,64},{64,96},{96,128},{128,160},{160,192},{192,224},{224... | collective-permute-start | bytes 1572872 | tf_op jit(solution)/shard_map/ppermute | solution.py:27
  21.8 28.4 %collective-permute-start.11 = (bf16[4096,256]{1,0:T(8,128)(2,1)S(1)}, bf16[4096,256]{1,0:T(8,128)(2,1)S(1)}, u32[]{:S(2)}, u32[]{:S(2)}) collective-permute-start(bf16[4096,256]{1,0:T(8,128)(2,1)S(1)} %constant_dynamic-update-slice_fusion.2.line), channel_id=1, source_target_pairs={{0,24},{1,7},{2,26},{3,1},{4,28},{5,3},{6,30},{7,5},{8,0},{9,15},{... | collective-permute-start | bytes 6291464 | tf_op jit(solution)/shard_map/ppermute | solution.py:41
  23.7 26.4 %collective-permute-start.7 = (bf16[4096,256]{1,0:T(8,128)(2,1)S(1)}, bf16[4096,256]{1,0:T(8,128)(2,1)S(1)}, u32[]{:S(2)}, u32[]{:S(2)}) collective-permute-start(bf16[4096,256]{1,0:T(8,128)(2,1)S(1)} %constant_dynamic-update-slice_fusion.2.line), channel_id=1, source_target_pairs={{0,8},{1,3},{2,10},{3,5},{4,12},{5,7},{6,14},{7,1},{8,16},{9,11},{... | collective-permute-start | bytes 6291464 | tf_op jit(solution)/shard_map/ppermute | solution.py:41
  25.4 13.4 %collective-permute-start.9 = (bf16[4,256,256]{2,1,0:T(8,128)(2,1)S(1)}, bf16[4,256,256]{2,1,0:T(8,128)(2,1)S(1)}, u32[]{:S(2)}, u32[]{:S(2)}) collective-permute-start(bf16[4,256,256]{2,1,0:T(8,128)(2,1)S(1)} %hold.9.refs_4_), channel_id=1, source_target_pairs={{0,224},{32,0},{64,32},{96,64},{128,96},{160,128},{192,160},{224,1... | collective-permute-start | bytes 1572872 | tf_op jit(solution)/shard_map/ppermute | solution.py:27
  29.1 13.1 %collective-permute-start.2 = (bf16[4,256,256]{2,1,0:T(8,128)(2,1)S(1)}, bf16[4,256,256]{2,1,0:T(8,128)(2,1)S(1)}, u32[]{:S(2)}, u32[]{:S(2)}) collective-permute-start(bf16[4,256,256]{2,1,0:T(8,128)(2,1)S(1)} %hold.6.refs_1_), channel_id=1, source_target_pairs={{0,32},{32,64},{64,96},{96,128},{128,160},{160,192},{192,224},{224... | collective-permute-start | bytes 1572872 | tf_op jit(solution)/shard_map/ppermute | solution.py:27
  38.8 14.3 %collective-permute-start.10 = (bf16[4,256,256]{2,1,0:T(8,128)(2,1)S(1)}, bf16[4,256,256]{2,1,0:T(8,128)(2,1)S(1)}, u32[]{:S(2)}, u32[]{:S(2)}) collective-permute-start(bf16[4,256,256]{2,1,0:T(8,128)(2,1)S(1)} %hold.10.refs_5_), channel_id=1, source_target_pairs={{0,224},{32,0},{64,32},{96,64},{128,96},{160,128},{192,160},{224,1... | collective-permute-start | bytes 1572872 | tf_op jit(solution)/shard_map/ppermute | solution.py:27
  42.2 11.9 %collective-permute-start.3 = (bf16[4,256,256]{2,1,0:T(8,128)(2,1)S(1)}, bf16[4,256,256]{2,1,0:T(8,128)(2,1)S(1)}, u32[]{:S(2)}, u32[]{:S(2)}) collective-permute-start(bf16[4,256,256]{2,1,0:T(8,128)(2,1)S(1)} %hold.7.refs_2_), channel_id=1, source_target_pairs={{0,32},{32,64},{64,96},{96,128},{128,160},{160,192},{192,224},{224... | collective-permute-start | bytes 1572872 | tf_op jit(solution)/shard_map/ppermute | solution.py:27
  50.1 20.3 %collective-permute-start.14 = (bf16[2048,256]{1,0:T(8,128)(2,1)S(1)}, bf16[2048,256]{1,0:T(8,128)(2,1)S(1)}, u32[]{:S(2)}, u32[]{:S(2)}) collective-permute-start(bf16[2048,256]{1,0:T(8,128)(2,1)S(1)} %slice.32), channel_id=1, source_target_pairs={{0,8},{1,3},{2,10},{3,5},{4,12},{5,7},{6,14},{7,1},{8,16},{9,11},{... | collective-permute-start | bytes 3145736 | tf_op jit(solution)/shard_map/ppermute | solution.py:41
  50.3 20.1 %collective-permute-start.15 = (bf16[2048,256]{1,0:T(8,128)(2,1)S(1)}, bf16[2048,256]{1,0:T(8,128)(2,1)S(1)}, u32[]{:S(2)}, u32[]{:S(2)}) collective-permute-start(bf16[2048,256]{1,0:T(8,128)(2,1)S(1)} %slice.33), channel_id=1, source_target_pairs={{0,24},{1,7},{2,26},{3,1},{4,28},{5,3},{6,30},{7,5},{8,0},{9,15},{... | collective-permute-start | bytes 3145736 | tf_op jit(solution)/shard_map/ppermute | solution.py:41
  54.1 7.7 %collective-permute-start.13 = (bf16[2,256,256]{2,1,0:T(8,128)(2,1)S(1)}, bf16[2,256,256]{2,1,0:T(8,128)(2,1)S(1)}, u32[]{:S(2)}, u32[]{:S(2)}) collective-permute-start(bf16[2,256,256]{2,1,0:T(8,128)(2,1)S(1)} %slice.25), channel_id=1, source_target_pairs={{0,224},{32,0},{64,32},{96,64},{128,96},{160,128},{192,160},{224,1... | collective-permute-start | bytes 786440 | tf_op jit(solution)/shard_map/ppermute | solution.py:27
  58.6 7.0 %collective-permute-start.12 = (bf16[2,256,256]{2,1,0:T(8,128)(2,1)S(1)}, bf16[2,256,256]{2,1,0:T(8,128)(2,1)S(1)}, u32[]{:S(2)}, u32[]{:S(2)}) collective-permute-start(bf16[2,256,256]{2,1,0:T(8,128)(2,1)S(1)} %slice.24), channel_id=1, source_target_pairs={{0,32},{32,64},{64,96},{96,128},{128,160},{160,192},{192,224},{224... | collective-permute-start | bytes 786440 | tf_op jit(solution)/shard_map/ppermute | solution.py:27
  66.5 4.0 %copy-start.1 = (s32[8,2]{0,1:T(2,128)S(1)}, s32[8,2]{0,1:T(2,128)}, u32[]{:S(2)}) copy-start(s32[8,2]{0,1:T(2,128)} %param.6) | copy-start | bytes 196
  66.5 4.0 %copy-start.2 = (s32[8]{0:T(128)S(1)}, s32[8]{0:T(128)}, u32[]{:S(2)}) copy-start(s32[8]{0:T(128)} %flag.3) | copy-start | bytes 100
  72.1 22.2 %collective-permute-start.16 = (f32[1024,256]{1,0:T(8,128)S(1)}, f32[1024,256]{1,0:T(8,128)S(1)}, u32[]{:S(2)}, u32[]{:S(2)}) collective-permute-start(f32[1024,256]{1,0:T(8,128)S(1)} %get-tuple-element.23), channel_id=1, source_target_pairs={{0,1},{1,0},{2,3},{3,2},{4,5},{5,4},{6,7},{7,6},{8,9},{9,8},{10,11... | collective-permute-start | bytes 3145736 | tf_op jit(solution)/shard_map/ppermute | solution.py:259
  90.9 5.6 %collective-permute-start.17 = (f32[8,128]{1,0:T(8,128)S(1)}, f32[8,128]{1,0:T(8,128)S(1)}, u32[]{:S(2)}, u32[]{:S(2)}) collective-permute-start(f32[8,128]{1,0:T(8,128)S(1)} %bitcast_reduce_fusion), channel_id=1, source_target_pairs={{0,2},{2,0},{4,6},{6,4},{1,3},{3,1},{5,7},{7,5},{8,10},{10,8},{12,... | collective-permute-start | bytes 12296 | tf_op jit(solution)/shard_map/ppermute | solution.py:203
  92.2 4.4 %collective-permute-start.18 = (f32[8,128]{1,0:T(8,128)S(1)}, f32[8,128]{1,0:T(8,128)S(1)}, u32[]{:S(2)}, u32[]{:S(2)}) collective-permute-start(f32[8,128]{1,0:T(8,128)S(1)} %bitcast_reduce_fusion), channel_id=1, source_target_pairs={{0,6},{2,4},{4,2},{6,0},{1,7},{3,5},{5,3},{7,1},{8,14},{10,12},{12... | collective-permute-start | bytes 12296 | tf_op jit(solution)/shard_map/ppermute | solution.py:203
  93.2 4.0 %collective-permute-start.19 = (f32[8,128]{1,0:T(8,128)S(1)}, f32[8,128]{1,0:T(8,128)S(1)}, u32[]{:S(2)}, u32[]{:S(2)}) collective-permute-start(f32[8,128]{1,0:T(8,128)S(1)} %bitcast_reduce_fusion), channel_id=1, source_target_pairs={{0,4},{2,6},{4,0},{6,2},{1,5},{3,7},{5,1},{7,3},{8,12},{10,14},{12... | collective-permute-start | bytes 12296 | tf_op jit(solution)/shard_map/ppermute | solution.py:203
